TPU v7x, 256 devices: a whole 4x4x8 slice. The times are simulated.
256 devices in a mesh: row: 8 (over x, y_hi), col: 8 (over z), dp: 4 (over y_lo, core).
Axes of the slice: x: 4, y: 4 (y_hi: 2, y_lo: 2; y = y_hi * 2 + y_lo), z: 8, core: 2. Of those that a mesh axis runs over, the one named last changes fastest.
Arguments:
- latent_image: bfloat16 [8, 448, 3072], P('dp', 'col'), may hold values from -127 to 127
- latent_text: bfloat16 [8, 64, 3072], P('dp', 'col'), may hold values from -127 to 127
- noise_image: bfloat16 [8, 448, 3072], P('dp', 'col'), may hold values from -5 to 5
- noise_text: bfloat16 [8, 64, 3072], P('dp', 'col'), may hold values from -5 to 5
- up_image: bfloat16 [3072, 12288], P('row', 'col'), may hold values from -0.109375 to 0.109375
- down_image: bfloat16 [3072, 12288], P('row', 'col'), may hold values from -0.0546875 to 0.0546875
- up_text: bfloat16 [3072, 12288], P('row', 'col'), may hold values from -0.109375 to 0.109375
- down_text: bfloat16 [3072, 12288], P('row', 'col'), may hold values from -0.0546875 to 0.0546875
- modulation: float32 [2, 3, 2, 3072], replicated, may hold values from -3 to 3
- timesteps: int32 [8], P('dp'), may hold values from 500 to 999
- skips: int32 [8], P('dp'), may hold values from 1 to 499
- text_lengths: int32 [8], P('dp'), may hold values from 1 to 64, 288 in all
Outputs:
- grad_up_image: float32 [3072, 12288], P('row', ('col', 'dp'))
- grad_down_image: float32 [3072, 12288], P('row', ('col', 'dp'))
- grad_up_text: float32 [3072, 12288], P('row', ('col', 'dp'))
- grad_down_text: float32 [3072, 12288], P('row', ('col', 'dp'))
All inputs are finite; a program needn't handle non-finite values. No bound on the sum of `text_lengths` on one device may be relied on, other than what follows from the above.
Results may differ from a plain program's by a relative error of at most 0.03.
Values may be sent and summed in bfloat16 or wider, within the bound.
A program may use at most 64 MiB of HBM per device.

v0:
```python
import math

import jax
import jax.numpy as jnp
from jax import lax
from jax.sharding import PartitionSpec as P

D = 3072
IMG = 448
STEPS = 1000
SEQ = 512


GELU_SCALE = 0.7978845608028654
GELU_CUBIC = 0.044715
NORM_EPS = 1e-06


def shortened(x):

    def short(part):
        return part.astype(jnp.bfloat16) if part.dtype == jnp.float32 else part

    return jax.tree.map(short, x)


def gelu_tanh(values):
    inner = GELU_SCALE * (values + GELU_CUBIC * values * values * values)
    return 0.5 * values * (1.0 + jnp.tanh(inner))


def gelu_slope(values):
    inner = GELU_SCALE * (values + GELU_CUBIC * values * values * values)
    tangent = jnp.tanh(inner)
    return 0.5 * (1.0 + tangent) + 0.5 * values * (1.0 - tangent * tangent) * GELU_SCALE * (
        1.0 + 3.0 * GELU_CUBIC * values * values
    )


def time_features(times_both, channels):
    half_width = channels // 2
    channel = jnp.arange(channels) % half_width
    frequency = jnp.exp(-math.log(10000.0) * channel.astype(jnp.float32) / half_width)
    angles = times_both[:, None] * frequency[None, :]
    return jnp.where(jnp.arange(channels)[None, :] < half_width, jnp.cos(angles), jnp.sin(angles))


def modulated_slice(noisy_input, mod_table, features, offset, slab_width):
    shift_rows = lax.dynamic_slice_in_dim(
        mod_table[0, 0] + mod_table[0, 1] * features, offset, slab_width, 1
    )
    scale_rows = lax.dynamic_slice_in_dim(
        mod_table[1, 0] + mod_table[1, 1] * features, offset, slab_width, 1
    )
    gate_rows = lax.dynamic_slice_in_dim(
        mod_table[2, 0] + mod_table[2, 1] * features, offset, slab_width, 1
    )
    row_mean = jnp.mean(noisy_input, axis=-1, keepdims=True)
    centered = noisy_input - row_mean
    variance = jnp.mean(centered * centered, axis=-1, keepdims=True)
    normed = lax.dynamic_slice_in_dim(centered, offset, slab_width, 2) * lax.rsqrt(
        variance + NORM_EPS
    )
    u_rows = (normed * (1.0 + scale_rows[:, None, :]) + shift_rows[:, None, :]).astype(jnp.bfloat16)
    return (u_rows, gate_rows, lax.dynamic_slice_in_dim(noisy_input, offset, slab_width, 2))


def gather_columns(panels):
    return (
        lax.all_gather(panels[0], "col", axis=1, tiled=True),
        lax.all_gather(panels[1], "col", axis=1, tiled=True),
    )


def share_rows(panels, weights):
    partials = tuple(
        (
            jnp.einsum("std,df->stf", panel_rows, weight_rows, preferred_element_type=jnp.float32)
            for panel_rows, weight_rows in zip(panels, weights)
        )
    )
    return jax.tree.map(
        lambda part: part.astype(jnp.float32),
        lax.psum_scatter(shortened(partials), "row", scatter_dimension=1, tiled=True),
    )


def gather_rows(shares):
    return jax.tree.map(
        lambda part, own: part.astype(own.dtype),
        lax.all_gather(shortened(shares), "row", axis=1, tiled=True),
        shares,
    )


def body(
    latent_image,
    latent_text,
    noise_image,
    noise_text,
    up_image,
    down_image,
    up_text,
    down_text,
    modulation,
    timesteps,
    skips,
    text_lengths,
):
    samples = timesteps.shape[0]
    slab_width = up_image.shape[0]
    offset = lax.axis_index("row") * slab_width
    total_samples = samples * lax.axis_size("dp")
    t_student = timesteps.astype(jnp.float32)
    t_target = (timesteps - skips).astype(jnp.float32)
    times_both = jnp.concatenate([t_student, t_target])
    features = time_features(times_both, D)
    noise_level = (times_both / STEPS)[:, None, None]
    weight_all = SEQ / math.sqrt(total_samples * SEQ) / (IMG + text_lengths).astype(jnp.float32)
    text_rows = latent_text.shape[1]
    positions = lax.axis_index("col") * text_rows + jnp.arange(text_rows)
    text_mask = (positions[None, :] < text_lengths[:, None]).astype(jnp.float32)
    image_mask = jnp.ones((samples, latent_image.shape[1]), jnp.float32)
    prepared = []
    for latent_rows, noise_rows, mod_table in (
        (latent_image, noise_image, modulation[0]),
        (latent_text, noise_text, modulation[1]),
    ):
        clean_part = latent_rows.astype(jnp.float32)
        noise_part = noise_rows.astype(jnp.float32)
        noisy_input = (1.0 - noise_level) * jnp.concatenate(
            [clean_part, clean_part]
        ) + noise_level * jnp.concatenate([noise_part, noise_part])
        prepared.append(modulated_slice(noisy_input, mod_table, features, offset, slab_width))
    panels = gather_columns((prepared[0][0], prepared[1][0]))
    pre_all = share_rows(panels, (up_image, up_text))
    pre_shares = tuple((share[:samples] for share in pre_all))
    hidden = gather_rows(tuple((gelu_tanh(share).astype(jnp.bfloat16) for share in pre_all)))
    out_terms = tuple(
        (
            jnp.einsum("stf,df->std", hid_rows, down_rows, preferred_element_type=jnp.float32)
            for hid_rows, down_rows in zip(hidden, (down_image, down_text))
        )
    )
    mlp_outs = jax.tree.map(
        lambda part: part.astype(jnp.float32),
        lax.psum_scatter(shortened(out_terms), "col", scatter_dimension=1, tiled=True),
    )
    errors = []
    for (u_rows, gate_rows, input_slice), mlp_out, mask_rows in zip(
        prepared, mlp_outs, (image_mask, text_mask)
    ):
        block_out = input_slice + gate_rows[:, None, :] * mlp_out
        out_grad = (
            weight_all[:, None, None]
            * mask_rows[:, :, None]
            * (block_out[:samples] - block_out[samples:])
        )
        errors.append((gate_rows[:samples][:, None, :] * out_grad).astype(jnp.bfloat16))
    err_panels = gather_columns((errors[0], errors[1]))
    back_sums = share_rows(err_panels, (down_image, down_text))
    slopes = tuple(
        (
            (back_share * gelu_slope(pre_share)).astype(jnp.bfloat16)
            for back_share, pre_share in zip(back_sums, pre_shares)
        )
    )
    slope_all = gather_rows(slopes)
    gradients = []
    for up_panel, err_panel, hid_rows, slope_rows in zip(panels, err_panels, hidden, slope_all):
        gradients.append(
            jnp.einsum(
                "std,stf->df", up_panel[:samples], slope_rows, preferred_element_type=jnp.float32
            )
        )
        gradients.append(
            jnp.einsum(
                "std,stf->df", err_panel, hid_rows[:samples], preferred_element_type=jnp.float32
            )
        )
    reduced = (
        lax.psum_scatter(
            gradients[0].astype(jnp.bfloat16), "dp", scatter_dimension=1, tiled=True
        ).astype(jnp.float32),
        lax.psum_scatter(
            gradients[1].astype(jnp.bfloat16), "dp", scatter_dimension=1, tiled=True
        ).astype(jnp.float32),
        lax.psum_scatter(
            gradients[2].astype(jnp.bfloat16), "dp", scatter_dimension=1, tiled=True
        ).astype(jnp.float32),
        lax.psum_scatter(
            gradients[3].astype(jnp.bfloat16), "dp", scatter_dimension=1, tiled=True
        ).astype(jnp.float32),
    )
    return (reduced[0], reduced[1], reduced[2], reduced[3])


def solution(mesh):
    placed = (
        P("dp", "col", None),
        P("dp", "col", None),
        P("dp", "col", None),
        P("dp", "col", None),
        P("row", "col"),
        P("row", "col"),
        P("row", "col"),
        P("row", "col"),
        P(),
        P("dp"),
        P("dp"),
        P("dp"),
    )
    return jax.shard_map(
        body,
        mesh=mesh,
        in_specs=placed,
        out_specs=(
            P("row", ("col", "dp")),
            P("row", ("col", "dp")),
            P("row", ("col", "dp")),
            P("row", ("col", "dp")),
        ),
        check_vma=False,
    )
```

profile of v0, /device:TPU:1, one launch (start us, length us, event | category | flops | bytes accessed | tf_op | source)
XLA Modules:
  0.0 768.6 jit_solution(6985700128479476221)
XLA Ops:
  8.1 3.9 fusion.54
  13.1 2.2 multiply_reduce_fusion
  16.6 39.4 %all-gather.4.cloned.1.call-done = bf16[4,448,384]{2,1,0:T(8,128)(2,1)} async-done(((bf16[4,56,384]{2,1,0:T(8,128)(2,1)}), bf16[4,448,384]{2,1,0:T(8,128)(2,1)}) %all-gather.4.cloned.1.call-update) | async-done | bytes 1376272 | tf_op jit(solution)/shard_map/all_gather | solution.py:70
  56.0 4.5 convolution_convert_fusion
  60.6 4.2 copy.16
  64.8 4.0 copy.36
  68.9 100.7 %reduce-scatter.31.cloned.1.call-done = bf16[56,6144]{1,0:T(8,128)(2,1)} async-done(((bf16[448,6144]{1,0:T(8,128)(2,1)}), bf16[56,6144]{1,0:T(8,128)(2,1)}) %reduce-scatter.31.cloned.1.call-update) | async-done | bytes 688144
  169.6 2.2 reshape.155
  173.8 20.7 %all_gather.28 = bf16[4,64,384]{2,1,0:T(8,128)(2,1)S(1)} all-gather(bf16[4,8,384]{2,1,0:T(8,128)(2,1)S(1)} %add_convert_fusion.1), channel_id=1, replica_groups=mesh['row'=8,'col'=8,'dp'=4] {'col'}, dimensions={1}, use_global_device_ids=true | all-gather | bytes 221184 | tf_op jit(solution)/shard_map/all_gather | solution.py:71
  196.7 63.1 %all-gather.6.cloned.1.call-done = bf16[4,448,1536]{2,1,0:T(8,128)(2,1)} async-done(((bf16[4,56,1536]{2,1,0:T(8,128)(2,1)}), bf16[4,448,1536]{2,1,0:T(8,128)(2,1)}) %all-gather.6.cloned.1.call-update) | async-done | bytes 5505040 | tf_op jit(solution)/shard_map/all_gather | solution.py:91
  259.8 5.6 convolution_convert_fusion.4
  268.5 69.1 %reduce-scatter.41.cloned.1.call-done = bf16[8,6144]{1,0:T(8,128)(2,1)} async-done(((bf16[64,6144]{1,0:T(8,128)(2,1)}), bf16[8,6144]{1,0:T(8,128)(2,1)}) %reduce-scatter.41.cloned.1.call-update) | async-done | bytes 98320
  338.6 30.0 %all_gather.29 = bf16[4,64,1536]{2,1,0:T(8,128)(2,1)S(1)} all-gather(bf16[4,8,1536]{2,1,0:T(8,128)(2,1)S(1)} %fusion.32), channel_id=1, replica_groups=mesh['row'=8,'col'=8,'dp'=4] {'row'}, dimensions={1}, use_global_device_ids=true | all-gather | bytes 884736 | tf_op jit(solution)/shard_map/all_gather | solution.py:91
  371.0 5.9 reduce-scatter.33.cloned.1.call-done
  378.9 20.3 %all_gather.26 = bf16[2,448,384]{2,1,0:T(8,128)(2,1)S(1)} all-gather(bf16[2,56,384]{2,1,0:T(8,128)(2,1)S(1)} %fusion.35), channel_id=1, replica_groups=mesh['row'=8,'col'=8,'dp'=4] {'col'}, dimensions={1}, use_global_device_ids=true | all-gather | bytes 774144 | tf_op jit(solution)/shard_map/all_gather | solution.py:70
  399.2 2.9 convolution_convert_fusion.1
  402.1 2.8 copy.20
  404.9 2.1 copy.38
  407.2 6.9 reduce-scatter.43.cloned.1.call-done
  415.0 18.6 %all_gather.30 = bf16[2,64,384]{2,1,0:T(8,128)(2,1)S(1)} all-gather(bf16[2,8,384]{2,1,0:T(8,128)(2,1)S(1)} %fusion.46), channel_id=1, replica_groups=mesh['row'=8,'col'=8,'dp'=4] {'col'}, dimensions={1}, use_global_device_ids=true | all-gather | bytes 110592 | tf_op jit(solution)/shard_map/all_gather | solution.py:71
  433.6 1.8 convolution_convert_fusion.3
  436.9 67.6 %reduce-scatter.35.cloned.1.call-done = bf16[56,3072]{1,0:T(8,128)(2,1)} async-done(((bf16[448,3072]{1,0:T(8,128)(2,1)}), bf16[56,3072]{1,0:T(8,128)(2,1)}) %reduce-scatter.35.cloned.1.call-update) | async-done | bytes 344080
  507.0 1.5 fusion
  510.1 73.9 %reduce-scatter.45.cloned.1.call-done = bf16[8,3072]{1,0:T(8,128)(2,1)} async-done(((bf16[64,3072]{1,0:T(8,128)(2,1)}), bf16[8,3072]{1,0:T(8,128)(2,1)}) %reduce-scatter.45.cloned.1.call-update) | async-done | bytes 49168
  584.9 28.9 %all_gather.31 = bf16[2,64,1536]{2,1,0:T(8,128)(2,1)S(1)} all-gather(bf16[2,8,1536]{2,1,0:T(8,128)(2,1)S(1)} %fusion.42), channel_id=1, replica_groups=mesh['row'=8,'col'=8,'dp'=4] {'row'}, dimensions={1}, use_global_device_ids=true | all-gather | bytes 442368 | tf_op jit(solution)/shard_map/all_gather | solution.py:91
  615.7 3.2 fusion.2
  620.4 33.0 %all-gather.8.cloned.1.call-done = bf16[2,448,1536]{2,1,0:T(8,128)(2,1)} async-done(((bf16[2,56,1536]{2,1,0:T(8,128)(2,1)}), bf16[2,448,1536]{2,1,0:T(8,128)(2,1)}) %all-gather.8.cloned.1.call-update) | async-done | bytes 2752528 | tf_op jit(solution)/shard_map/all_gather | solution.py:91
  653.4 3.2 fusion.3
  658.1 21.0 %reduce-scatter.49.cloned.1.call-done = bf16[384,384]{1,0:T(8,128)(2,1)} async-done(((bf16[1536,384]{1,0:T(8,128)(2,1)}), bf16[384,384]{1,0:T(8,128)(2,1)}) %reduce-scatter.49.cloned.1.call-update) | async-done | bytes 294928
  681.1 25.1 %reduce-scatter.47.cloned.1.call-done = bf16[384,384]{1,0:T(8,128)(2,1)} async-done(((bf16[1536,384]{1,0:T(8,128)(2,1)}), bf16[384,384]{1,0:T(8,128)(2,1)}) %reduce-scatter.47.cloned.1.call-update) | async-done | bytes 294928
  708.1 24.9 %reduce-scatter.39.cloned.1.call-done = bf16[384,384]{1,0:T(8,128)(2,1)} async-done(((bf16[1536,384]{1,0:T(8,128)(2,1)}), bf16[384,384]{1,0:T(8,128)(2,1)}) %reduce-scatter.39.cloned.1.call-update) | async-done | bytes 294928
  735.1 24.9 %reduce-scatter.37.cloned.1.call-done = bf16[384,384]{1,0:T(8,128)(2,1)} async-done(((bf16[1536,384]{1,0:T(8,128)(2,1)}), bf16[384,384]{1,0:T(8,128)(2,1)}) %reduce-scatter.37.cloned.1.call-update) | async-done | bytes 294928
  (124 shorter events, 36.4 us)
Async XLA Ops:
  7.2 48.8 %copy-start = (bf16[384,1536]{1,0:T(8,128)(2,1)S(1)}, bf16[384,1536]{1,0:T(8,128)(2,1)}, u32[]{:S(2)}) copy-start(bf16[384,1536]{1,0:T(8,128)(2,1)} %param.16) | copy-start | bytes 3538948
  7.2 48.8 %all-gather.4.cloned.1.call-start = ((), (), s32[]{:S(2)}) async-start(), calls=%async_computation.10 | async-start | bytes 1548288 | tf_op jit(solution)/shard_map/all_gather | solution.py:70
  8.1 3.9 copy-start.8
  16.6 153.0 %reduce-scatter.31.cloned.1.call-start = ((), (), s32[]{:S(2)}) async-start(), calls=%async_computation.13 | async-start | bytes 6193152
  68.9 190.9 %all-gather.6.cloned.1.call-start = ((), (), s32[]{:S(2)}) async-start(), calls=%async_computation.11 | async-start | bytes 6193152 | tf_op jit(solution)/shard_map/all_gather | solution.py:91
  171.8 1.4 copy-start.9
  171.8 1.4 copy-start.10
  173.1 21.3 %copy-start.4 = (bf16[384,1536]{1,0:T(8,128)(2,1)S(1)}, bf16[384,1536]{1,0:T(8,128)(2,1)}, u32[]{:S(2)}) copy-start(bf16[384,1536]{1,0:T(8,128)(2,1)} %param.18) | copy-start | bytes 3538948
  173.1 164.4 %reduce-scatter.41.cloned.1.call-start = ((), (), s32[]{:S(2)}) async-start(), calls=%async_computation.18 | async-start | bytes 884736
  195.6 64.2 %copy-start.12 = (bf16[384,1536]{1,0:T(8,128)(2,1)S(1)}, bf16[384,1536]{1,0:T(8,128)(2,1)}, u32[]{:S(2)}) copy-start(bf16[384,1536]{1,0:T(8,128)(2,1)} %param.17) | copy-start | bytes 3538948
  196.7 180.2 %reduce-scatter.33.cloned.1.call-start = ((), (), s32[]{:S(2)}) async-start(), calls=%async_computation.14 | async-start | bytes 1548288
  267.8 0.7 copy-start.11
  267.8 101.6 %copy-start.3 = (bf16[384,1536]{1,0:T(8,128)(2,1)S(1)}, bf16[384,1536]{1,0:T(8,128)(2,1)}, u32[]{:S(2)}) copy-start(bf16[384,1536]{1,0:T(8,128)(2,1)} %param.19) | copy-start | bytes 3538948
  267.8 146.4 %reduce-scatter.43.cloned.1.call-start = ((), (), s32[]{:S(2)}) async-start(), calls=%async_computation.19 | async-start | bytes 221184
  338.5 31.5 %copy-start.5 = (bf16[8,4,1536]{2,1,0:T(4,128)(2,1)}, bf16[8,4,1536]{2,1,0:T(4,128)(2,1)S(1)}, u32[]{:S(2)}) copy-start(bf16[8,4,1536]{2,1,0:T(4,128)(2,1)S(1)} %reshape.165) | copy-start | bytes 294916
  368.6 0.9 copy-start.2
  370.9 133.6 %reduce-scatter.35.cloned.1.call-start = ((), (), s32[]{:S(2)}) async-start(), calls=%async_computation.15 | async-start | bytes 3096576
  407.1 176.9 %reduce-scatter.45.cloned.1.call-start = ((), (), s32[]{:S(2)}) async-start(), calls=%async_computation.20 | async-start | bytes 442368
  436.7 216.8 %all-gather.8.cloned.1.call-start = ((), (), s32[]{:S(2)}) async-start(), calls=%async_computation.12 | async-start | bytes 3096576 | tf_op jit(solution)/shard_map/all_gather | solution.py:91
  507.0 172.1 %reduce-scatter.49.cloned.1.call-start = ((), (), s32[]{:S(2)}) async-start(), calls=%async_computation.22 | async-start | bytes 1474560
  508.5 1.5 copy-start.6
  510.0 196.1 %reduce-scatter.47.cloned.1.call-start = ((), (), s32[]{:S(2)}) async-start(), calls=%async_computation.21 | async-start | bytes 1474560
  615.7 117.3 %reduce-scatter.39.cloned.1.call-start = ((), (), s32[]{:S(2)}) async-start(), calls=%async_computation.17 | async-start | bytes 1474560
  618.9 34.5 %copy-start.7 = (bf16[4,448,384]{2,1,0:T(8,128)(2,1)S(1)}, bf16[4,448,384]{2,1,0:T(8,128)(2,1)}, u32[]{:S(2)}) copy-start(bf16[4,448,384]{2,1,0:T(8,128)(2,1)} %all-gather.4.cloned.1.call-done) | copy-start | bytes 4128772
  620.4 139.6 %reduce-scatter.37.cloned.1.call-start = ((), (), s32[]{:S(2)}) async-start(), calls=%async_computation.16 | async-start | bytes 1474560
  733.0 29.1 %copy-start.1 = (bf16[384,1536]{1,0:T(8,128)(2,1)S(1)}, bf16[384,1536]{1,0:T(8,128)(2,1)}, u32[]{:S(2)}) copy-start(bf16[384,1536]{1,0:T(8,128)(2,1)} %param.16) | copy-start | bytes 3538948
Sparse Core Ops, SparseCore 0:
  16.7 39.2 all-gather.3
  69.0 100.5 reduce-scatter.30
  173.3 86.4 all-gather.5
  264.1 73.4 reduce-scatter.40
  340.1 36.7 reduce-scatter.32
  379.8 34.3 reduce-scatter.42
  418.9 85.5 reduce-scatter.34
  509.5 74.4 reduce-scatter.44
  587.5 65.8 all-gather.7
  656.0 22.9 reduce-scatter.48
  681.8 24.2 reduce-scatter.46
  708.7 24.2 reduce-scatter.38
  735.7 24.2 reduce-scatter.36
where the time goes:
time: 769 us
  waiting for transfers between devices  556 us (72%)
  blocking collectives  118 us (15%)
  local copies, waits for them, and re-layouts  39.1 us (5%)
  matrix products  24.3 us (3%)
  other arithmetic  16.4 us (2%)
  between operations  14.3 us (2%)
    unnamed x23, waiting for transfers between devices  420 us
    all_gather x2, waiting for transfers between devices, gather_rows(): lax.all_gather(shortened(shares), 'row', axis=1, tiled=True)  96.1 us
    all_gather x2, blocking collectives, gather_rows(): lax.all_gather(shortened(shares), 'row', axis=1, tiled=True)  58.8 us
    all_gather x1, waiting for transfers between devices, gather_columns(): lax.all_gather(panels[0], 'col', axis=1, tiled=True)  39.4 us
    all_gather x2, blocking collectives, gather_columns(): lax.all_gather(panels[1], 'col', axis=1, tiled=True)  39.2 us
    unnamed x52, local copies, waits for them, and re-layouts  38.1 us
    all_gather x1, blocking collectives, gather_columns(): lax.all_gather(panels[0], 'col', axis=1, tiled=True)  20.3 us
  transfers between devices with their start and end apart: 13, of which 13 were waited for; matrix products, arithmetic and copies ran while one was open for 7% of the time, Pallas kernels for 0%

commit v1 on v0

v1 whole, which is shorter than its diff:
```python
import functools
import math

import jax
import jax.numpy as jnp
from jax import lax
from jax.experimental import pallas as pl
from jax.experimental.pallas import tpu as pltpu
from jax.sharding import PartitionSpec as P

D = 3072
FF = 12288
IMG = 448
TXT = 64
STEPS = 1000
SEQ = 512

NX = 4
NZ = 8
CH = D // NX
HB = FF // NZ
HQ = HB // NX
RI = IMG // NZ
RT = TXT // NZ
NJ = 3
HJ = HQ // NJ
ROWS = D // 8
QR = ROWS // 4

GELU_SCALE = 0.7978845608028654
GELU_CUBIC = 0.044715
NORM_EPS = 1e-06
MESH = pl.DeviceIdType.MESH
F32 = jnp.float32
BF16 = jnp.bfloat16


def gelu_tanh(values):
    inner = GELU_SCALE * (values + GELU_CUBIC * values * values * values)
    return 0.5 * values * (1.0 + jnp.tanh(inner))


def gelu_slope(values):
    inner = GELU_SCALE * (values + GELU_CUBIC * values * values * values)
    tangent = jnp.tanh(inner)
    return 0.5 * (1.0 + tangent) + 0.5 * values * (1.0 - tangent * tangent) * GELU_SCALE * (
        1.0 + 3.0 * GELU_CUBIC * values * values
    )


def dot(a, b):
    return jnp.dot(a, b, preferred_element_type=F32)


def dot_nt(a, b):
    return lax.dot_general(a, b, (((1,), (1,)), ((), ())), preferred_element_type=F32)


def kernel(
    lat_i, lat_t, noi_i, noi_t, up_i, up_t, dn_i, dn_t, mod, coef, levels,
    out_ui, out_di, out_ut, out_dt,
    lbi, lbt, nbi, nbt, W, uimg, utxt, ndiff, u32,
    stg, stgt, rrs, rrst, hid, hidt, pre_c, h32, hc,
    zst, rem, zr, errz, e32, ec, uT, eT, uTt, eTt, hgs, hgr, pg, G, CR, YR,
    s_loc, s_wl, s_w1s, s_w1r, s_w2s, s_w2r, s_w3s, s_w3r,
    s_zis, s_zir, s_zts, s_ztr,
    s_rss, s_rsr, s_ags, s_agr, s_mzs, s_mzr, s_mrs, s_mrr, s_ezs, s_ezr,
    s_hgs, s_hgr, s_pgs, s_pgr, s_cs, s_cr, s_ys, s_yr,
):
    r = lax.axis_index("row")
    z = lax.axis_index("col")
    d = lax.axis_index("dp")
    x, hi, lo, c = r // 2, r % 2, d // 2, d % 2
    y = hi * 2 + lo

    def dev(x, hi, lo, c, z):
        return (x * 2 + hi, z, lo * 2 + c)

    def xdev(t):
        return dev((x + t) % NX, hi, lo, c, z)

    def zdev(t):
        return dev(x, hi, lo, c, (z + t + NZ) % NZ)

    def ydev(t):
        yy = (y + t) % 4
        return dev(x, yy // 2, yy % 2, c, z)

    core = dev(x, hi, lo, 1 - c, z)
    adj = dev(x, 1 - hi, 1 - lo, c, z)
    side = dev(x, hi, 1 - lo, c, z)

    def remote(src, dst, ss, rs, who):
        return pltpu.make_async_remote_copy(
            src_ref=src, dst_ref=dst, send_sem=ss, recv_sem=rs, device_id=who, device_id_type=MESH
        )

    bar = pltpu.get_barrier_semaphore()
    for t in range(1, NX):
        pl.semaphore_signal(bar, inc=1, device_id=xdev(t), device_id_type=MESH)
    for t in range(1, NZ):
        pl.semaphore_signal(bar, inc=1, device_id=zdev(t), device_id_type=MESH)
    for t in range(1, 4):
        pl.semaphore_signal(bar, inc=1, device_id=ydev(t), device_id_type=MESH)
    pl.semaphore_signal(bar, inc=1, device_id=core, device_id_type=MESH)

    reads = [
        pltpu.make_async_copy(lat_i.at[hi], lbi, s_loc.at[0]),
        pltpu.make_async_copy(lat_t.at[hi], lbt, s_loc.at[1]),
        pltpu.make_async_copy(noi_i.at[hi], nbi, s_loc.at[2]),
        pltpu.make_async_copy(noi_t.at[hi], nbt, s_loc.at[3]),
    ]
    for cp in reads:
        cp.start()
    weights = (up_i, up_t, dn_i, dn_t)
    wl = [
        pltpu.make_async_copy(
            weights[m], W.at[m, pl.ds(pl.multiple_of(hi * ROWS, ROWS), ROWS)], s_wl.at[m]
        )
        for m in range(4)
    ]

    pl.semaphore_wait(bar, 14)

    def wrows(m, half, quarter):
        return W.at[m, pl.ds(pl.multiple_of(half * ROWS + quarter * QR, QR), QR)]

    q_mine = lo * 2 + c
    q_side = (1 - lo) * 2 + c
    w1 = [
        remote(
            weights[m].at[pl.ds(pl.multiple_of(q_side * QR, QR), QR)],
            wrows(m, hi, q_side), s_w1s.at[m], s_w1r.at[m], adj,
        )
        for m in range(4)
    ]
    w1in = [remote(wrows(m, 1 - hi, q_mine), wrows(m, 1 - hi, q_mine), s_w1s.at[m], s_w1r.at[m], adj) for m in range(4)]
    w2 = [remote(wrows(m, 1 - hi, q_mine), wrows(m, 1 - hi, q_mine), s_w2s.at[m], s_w2r.at[m], side) for m in range(4)]
    w2in = [remote(wrows(m, 1 - hi, q_side), wrows(m, 1 - hi, q_side), s_w2s.at[m], s_w2r.at[m], side) for m in range(4)]
    w3a = [remote(wrows(m, 1 - hi, q_mine), wrows(m, 1 - hi, q_mine), s_w3s.at[m, 0], s_w3r.at[m, 0], core) for m in range(4)]
    w3b = [remote(wrows(m, 1 - hi, q_side), wrows(m, 1 - hi, q_side), s_w3s.at[m, 1], s_w3r.at[m, 1], core) for m in range(4)]

    def w_step1(m):
        w1in[m].wait_recv()
        w2[m].start()
        w3a[m].start()

    def w_step2(m):
        w2in[m].wait_recv()
        w3b[m].start()

    def w_step3(m):
        wl[m].wait()
        w3a[m].wait_recv()
        w3b[m].wait_recv()

    for m in range(4):
        w1[m].start()
    for m in range(4):
        wl[m].start()

    for cp in reads:
        cp.wait()
    lane0 = pl.multiple_of(x * CH, CH)
    for latb, noib, rows, stream, base in ((lbi, nbi, RI, 0, 0), (lbt, nbt, RT, 1, RI)):
        lat_own = latb[:, pl.ds(lane0, CH)].astype(F32)
        noi_own = noib[:, pl.ds(lane0, CH)].astype(F32)
        owns = []
        us = []
        for b in range(2):
            level = levels[b]
            full = (1.0 - level) * latb[...].astype(F32) + level * noib[...].astype(F32)
            mean = jnp.mean(full, axis=-1, keepdims=True)
            cen = full - mean
            var = jnp.mean(cen * cen, axis=-1, keepdims=True)
            own = (1.0 - level) * lat_own + level * noi_own
            owns.append(own)
            normed = (own - mean) * lax.rsqrt(var + NORM_EPS)
            us.append(normed * (1.0 + mod[stream, 1, b : b + 1, :]) + mod[stream, 0, b : b + 1, :])
        ndiff[base : base + rows, :] = owns[0] - owns[1]
        both = jnp.concatenate(us, axis=0).astype(BF16)
        if stream == 0:
            uimg[0] = both
        else:
            utxt[0:16, :] = both

    def send_z(i, to, who):
        a = remote(uimg.at[i], uimg.at[to], s_zis.at[to], s_zir.at[to], who)
        b = remote(
            utxt.at[pl.ds(pl.multiple_of(i * 16, 16), 16)],
            utxt.at[pl.ds(pl.multiple_of(to * 16, 16), 16)],
            s_zts.at[to], s_ztr.at[to], who,
        )
        return a, b

    for to, who in ((1, zdev(1)), (2, zdev(-1))):
        for cp in send_z(0, to, who):
            cp.start()

    w_step1(0)
    w_step1(1)
    w_step2(0)
    w_step3(0)

    def rs_img(i, t):
        return remote(stg.at[i, (x + t) % NX], rrs.at[i, t - 1], s_rss.at[i, t - 1], s_rsr.at[i, t - 1], xdev(t))

    def ag_img(i, t):
        return remote(hid.at[i, x], hid.at[i, x], s_ags.at[i, t - 1], s_agr.at[i, t - 1], xdev(t))

    def ag_img_in(i, t):
        f = (x + NX - t) % NX
        return remote(hid.at[i, f], hid.at[i, f], s_ags.at[i, t - 1], s_agr.at[i, t - 1], xdev(t))

    def rs_txt(t):
        return remote(stgt.at[(x + t) % NX], rrst.at[t - 1], s_rss.at[8, t - 1], s_rsr.at[8, t - 1], xdev(t))

    def ag_txt(t):
        return remote(hidt.at[x], hidt.at[x], s_ags.at[8, t - 1], s_agr.at[8, t - 1], xdev(t))

    def ag_txt_in(t):
        f = (x + NX - t) % NX
        return remote(hidt.at[f], hidt.at[f], s_ags.at[8, t - 1], s_agr.at[8, t - 1], xdev(t))

    def up_chunk(i, _):
        @pl.when(i > 0)
        def _():
            a, b = send_z(i, i, zdev(1))
            a.wait_recv()
            b.wait_recv()

        @pl.when(jnp.logical_and(i > 0, i < 6))
        def _():
            for cp in send_z(i, i + 2, zdev((i % 2) * 2 - 1)):
                cp.start()

        u = uimg[i]
        for q in range(NX):
            stg[i, q] = dot(u, W[0, :, q * HQ : (q + 1) * HQ]).astype(BF16)
        for t in range(1, NX):
            rs_img(i, t).start()
        return 0

    lax.fori_loop(0, NZ, up_chunk, 0)

    w_step2(1)
    w_step3(1)
    for q in range(NX):
        stgt[q] = dot(utxt[...], W[1, :, q * HQ : (q + 1) * HQ]).astype(BF16)
    for t in range(1, NX):
        rs_txt(t).start()
    w_step1(2)
    w_step1(3)
    w_step2(2)
    w_step2(3)

    def pack_u(i, _):
        u32[pl.ds(pl.multiple_of(i * RI, 8), RI), :] = uimg[i].astype(F32)[0:RI]
        u32[pl.ds(pl.multiple_of(IMG + i * RT, 8), RT), :] = utxt[
            pl.ds(pl.multiple_of(i * 16, 16), 16), :
        ].astype(F32)[0:RT]
        return 0

    lax.fori_loop(0, NZ, pack_u, 0)

    def act_chunk(i, _):
        for t in range(1, NX):
            rs_img(i, t).wait_recv()
        pre = stg[i, x].astype(F32)
        for t in range(1, NX):
            pre = pre + rrs[i, t - 1].astype(F32)
        pre_c[pl.ds(pl.multiple_of(i * RI, 8), RI), :] = pre[0:RI]
        hid[i, x] = gelu_tanh(pre).astype(BF16)
        for t in range(1, NX):
            ag_img(i, t).start()
        return 0

    def act_text():
        for t in range(1, NX):
            rs_txt(t).wait_recv()
        pre = stgt[x].astype(F32)
        for t in range(1, NX):
            pre = pre + rrst[t - 1].astype(F32)
        for i in range(NZ):
            pre_c[IMG + i * RT : IMG + (i + 1) * RT, :] = pre[i * 16 : i * 16 + RT]
        hidt[x] = gelu_tanh(pre).astype(BF16)
        for t in range(1, NX):
            ag_txt(t).start()

    lax.fori_loop(0, 6, act_chunk, 0)
    act_text()
    lax.fori_loop(6, NZ, act_chunk, 0)

    w_step3(2)
    w_step3(3)

    def zslot(i):
        half = (i + 1) // 2
        return (NZ + half - 2 * half * (i % 2)) % NZ

    def mz_main(i):
        s = zslot(i)
        return remote(zst.at[i, 0:48], zr.at[s, 0:48], s_mzs.at[i], s_mzr.at[s], zdev(s))

    def mz_rest(i):
        s = zslot(i)
        return remote(zst.at[i, 48:64], zr.at[s, 48:64], s_mrs.at[i], s_mrr.at[s], zdev(s))

    def down_chunk(i, _):
        for t in range(1, NX):
            ag_img_in(i, t).wait_recv()
        out = dot_nt(hid[i, 0], W[2, :, 0:HQ])
        for q in range(1, NX):
            out = out + dot_nt(hid[i, q], W[2, :, q * HQ : (q + 1) * HQ])
        diff = mod[0, 2, 0:1, :] * out[0:RI] - mod[0, 2, 1:2, :] * out[RI : 2 * RI]
        zst[i, 0:48, :] = diff[0:48].astype(BF16)
        rem[i, 0:8, :] = diff[48:56]

        @pl.when(i > 0)
        def _():
            mz_main(i).start()

        for q in range(NX):
            h32[q, pl.ds(pl.multiple_of(i * RI, 8), RI), :] = hid[i, q].astype(F32)[0:RI]
        return 0

    def rest_chunk(i, _):
        zst[i, 48:64, :] = rem[i].astype(BF16)

        @pl.when(i > 0)
        def _():
            mz_rest(i).start()

        return 0

    def down_text():
        for t in range(1, NX):
            ag_txt_in(t).wait_recv()
        out = dot_nt(hidt[0], W[3, :, 0:HQ])
        for q in range(1, NX):
            out = out + dot_nt(hidt[q], W[3, :, q * HQ : (q + 1) * HQ])
        for i in range(NZ):
            rem[i, 8:16, :] = (
                mod[1, 2, 0:1, :] * out[i * 16 : i * 16 + RT] - mod[1, 2, 1:2, :] * out[i * 16 + RT : (i + 1) * 16]
            )
        for q in range(NX):
            full = hidt[q].astype(F32)
            for i in range(NZ):
                h32[q, IMG + i * RT : IMG + (i + 1) * RT, :] = full[i * 16 : i * 16 + RT]

    lax.fori_loop(0, 6, down_chunk, 0)
    down_text()
    lax.fori_loop(0, 6, rest_chunk, 0)
    lax.fori_loop(6, NZ, down_chunk, 0)
    lax.fori_loop(6, NZ, rest_chunk, 0)

    img_lane = lax.broadcasted_iota(jnp.int32, (CH, SEQ), 1) < IMG
    txt_lane = lax.broadcasted_iota(jnp.int32, (CH, 128), 1) >= 64
    turned = u32[...].T
    uT[...] = jnp.where(img_lane, turned, 0.0).astype(BF16)
    uTt[...] = jnp.where(txt_lane, turned[:, SEQ - 128 :], 0.0).astype(BF16)
    hc[...] = h32[...].astype(BF16)

    total = ndiff[...] + zst[0].astype(F32)
    for s in range(1, NZ):
        a = remote(zst.at[s, 0:48], zr.at[s, 0:48], s_mzs.at[s], s_mzr.at[s], zdev(s))
        b = remote(zst.at[s, 48:64], zr.at[s, 48:64], s_mrs.at[s], s_mrr.at[s], zdev(s))
        a.wait_recv()
        b.wait_recv()
        total = total + zr[s].astype(F32)
    total = total * coef[:, 0:1]
    err_i = mod[0, 2, 0:1, :] * total[0:RI]
    err_t = mod[1, 2, 0:1, :] * total[RI : RI + RT]
    errz[0] = jnp.concatenate([err_i, err_t], axis=0).astype(BF16)

    def send_e(i, to, who):
        return remote(errz.at[i], errz.at[to], s_ezs.at[to], s_ezr.at[to], who)

    send_e(0, 1, zdev(1)).start()
    send_e(0, 2, zdev(-1)).start()

    def err_chunk(i, _):
        @pl.when(i > 0)
        def _():
            send_e(i, i, zdev(1)).wait_recv()

        @pl.when(jnp.logical_and(i > 0, i < 6))
        def _():
            send_e(i, i + 2, zdev((i % 2) * 2 - 1)).start()

        full = errz[i].astype(F32)
        e32[pl.ds(pl.multiple_of(i * RI, 8), RI), :] = full[0:RI]
        e32[pl.ds(pl.multiple_of(IMG + i * RT, 8), RT), :] = full[RI : RI + RT]
        return 0

    lax.fori_loop(0, NZ, err_chunk, 0)
    ec[...] = e32[...].astype(BF16)

    def hg_block(q, _):
        lanes = pl.ds(pl.multiple_of(q * HQ, HQ), HQ)
        gi = dot(ec[0:IMG], W[2, :, lanes]).astype(BF16)
        gt = dot(ec[IMG:SEQ], W[3, :, lanes]).astype(BF16)
        for j in range(NJ):
            hgs[j, q, 0:IMG, :] = gi[:, j * HJ : (j + 1) * HJ]
            hgs[j, q, IMG:SEQ, :] = gt[:, j * HJ : (j + 1) * HJ]
        return 0

    lax.fori_loop(0, NX, hg_block, 0)

    def rs_hg(j, t):
        return remote(hgs.at[j, (x + t) % NX], hgr.at[j, t - 1], s_hgs.at[j, t - 1], s_hgr.at[j, t - 1], xdev(t))

    for j in range(NJ):
        for t in range(1, NX):
            rs_hg(j, t).start()

    turned = e32[...].T
    eT[...] = jnp.where(img_lane, turned, 0.0).astype(BF16)
    eTt[...] = jnp.where(txt_lane, turned[:, SEQ - 128 :], 0.0).astype(BF16)

    def gd_block(q, _):
        G[0, q] = dot(eT[...], hc[q]).astype(BF16)
        G[1, q] = dot(eTt[...], hc[q, SEQ - 128 :, :]).astype(BF16)
        return 0

    lax.fori_loop(0, NX, gd_block, 0)

    def cols(m, j):
        return pl.ds(0, HQ) if j is None else pl.ds(j * HJ, HJ)

    def core_cp(p, m, j, l):
        return remote(
            G.at[m, l * 2 + 1 - c, :, cols(m, j)], CR.at[m, l, :, cols(m, j)], s_cs.at[p, l], s_cr.at[p, l], core
        )

    def y_cp(p, m, j, t):
        yy = (y + t) % 4
        rows = pl.ds(pl.multiple_of((yy // 2) * ROWS, ROWS), ROWS)
        return remote(
            G.at[m, (yy % 2) * 2 + c, rows, cols(m, j)], YR.at[m, t - 1, :, cols(m, j)],
            s_ys.at[p, t - 1], s_yr.at[p, t - 1], ydev(t),
        )

    def after_core(p, m, j):
        for l in range(2):
            core_cp(p, m, j, l).wait_recv()
            G[m, l * 2 + c, :, cols(m, j)] = (
                G[m, l * 2 + c, :, cols(m, j)].astype(F32) + CR[m, l, :, cols(m, j)].astype(F32)
            ).astype(BF16)
        for t in range(1, 4):
            y_cp(p, m, j, t).start()

    for m in range(2):
        for l in range(2):
            core_cp(m, m, None, l).start()

    def pre_grad(j):
        for t in range(1, NX):
            rs_hg(j, t).wait_recv()
        g = hgs[j, x].astype(F32)
        for t in range(1, NX):
            g = g + hgr[j, t - 1].astype(F32)
        own = (g * gelu_slope(pre_c[:, j * HJ : (j + 1) * HJ])).astype(BF16)
        pg[j, x] = own
        for t in range(1, NX):
            ag_pg(j, t).start()

    def ag_pg(j, t):
        return remote(pg.at[j, x], pg.at[j, x], s_pgs.at[j, t - 1], s_pgr.at[j, t - 1], xdev(t))

    def ag_pg_in(j, t):
        f = (x + NX - t) % NX
        return remote(pg.at[j, f], pg.at[j, f], s_pgs.at[j, t - 1], s_pgr.at[j, t - 1], xdev(t))

    pre_grad(0)
    after_core(0, 0, None)
    after_core(1, 1, None)
    for j in range(1, NJ):
        pre_grad(j)

    for j in range(NJ):
        for t in range(1, NX):
            ag_pg_in(j, t).wait_recv()
        wide = jnp.concatenate([pg[j, q] for q in range(NX)], axis=1)
        gi = dot(uT[...], wide).astype(BF16)
        gt = dot(uTt[...], wide[SEQ - 128 :]).astype(BF16)
        for q in range(NX):
            G[2, q, :, j * HJ : (j + 1) * HJ] = gi[:, q * HJ : (q + 1) * HJ]
            G[3, q, :, j * HJ : (j + 1) * HJ] = gt[:, q * HJ : (q + 1) * HJ]
        for k in range(2):
            for l in range(2):
                core_cp(2 + 2 * j + k, 2 + k, j, l).start()
        for k in range(2):
            after_core(2 + 2 * j + k, 2 + k, j)

    mine = pl.ds(pl.multiple_of(hi * ROWS, ROWS), ROWS)

    def finish(p, m, j, out):
        for t in range(1, 4):
            y_cp(p, m, j, t).wait_recv()
        g = G[m, lo * 2 + c, mine, cols(m, j)].astype(F32)
        for t in range(3):
            g = g + YR[m, t, :, cols(m, j)].astype(F32)
        out[:, cols(m, j)] = g

    finish(0, 0, None, out_di)
    finish(1, 1, None, out_dt)
    for j in range(NJ):
        finish(2 + 2 * j, 2, j, out_ui)
        finish(3 + 2 * j, 3, j, out_ut)

    for m in range(4):
        w1[m].wait_send()
        w2[m].wait_send()
        w3a[m].wait_send()
        w3b[m].wait_send()

    def sent(i, _):
        @pl.when(i > 0)
        def _():
            a, b = send_z(i, i, zdev(1))
            a.wait_send()
            b.wait_send()
            send_e(i, i, zdev(1)).wait_send()
            mz_main(i).wait_send()
            mz_rest(i).wait_send()

        for t in range(1, NX):
            rs_img(i, t).wait_send()
            ag_img(i, t).wait_send()
        return 0

    lax.fori_loop(0, NZ, sent, 0)
    for t in range(1, NX):
        rs_txt(t).wait_send()
        ag_txt(t).wait_send()
        for j in range(NJ):
            rs_hg(j, t).wait_send()
            ag_pg(j, t).wait_send()
    parts = [(0, 0, None), (1, 1, None)] + [(2 + 2 * j + k, 2 + k, j) for j in range(NJ) for k in range(2)]
    for p, m, j in parts:
        for l in range(2):
            core_cp(p, m, j, l).wait_send()
        for t in range(1, 4):
            y_cp(p, m, j, t).wait_send()


def body(
    latent_image, latent_text, noise_image, noise_text, up_image, down_image, up_text, down_text,
    modulation, timesteps, skips, text_lengths,
):
    r = lax.axis_index("row")
    x, hi = r // 2, r % 2
    total_samples = timesteps.shape[0] * lax.axis_size("dp")
    t_s = lax.dynamic_index_in_dim(timesteps, hi, 0, False)
    t_g = t_s - lax.dynamic_index_in_dim(skips, hi, 0, False)
    length = lax.dynamic_index_in_dim(text_lengths, hi, 0, False)
    times = jnp.stack([t_s, t_g]).astype(F32)
    half = D // 2
    channel = x * CH + jnp.arange(CH)
    frequency = jnp.exp(-math.log(10000.0) * (channel % half).astype(F32) / half)
    angles = times[:, None] * frequency[None, :]
    features = jnp.where(x < NX // 2, jnp.cos(angles), jnp.sin(angles))
    table = lax.dynamic_slice_in_dim(modulation, x * CH, CH, 3)
    mod = table[:, :, 0][:, :, None, :] + table[:, :, 1][:, :, None, :] * features
    levels = times / STEPS
    weight = SEQ / math.sqrt(total_samples * SEQ) / (IMG + length).astype(F32)
    row = jnp.arange(RI + RT)
    position = lax.axis_index("col") * RT + row - RI
    coef = jnp.where(jnp.logical_or(row < RI, position < length), weight, 0.0)
    coef = jnp.broadcast_to(coef[:, None], (RI + RT, 128))

    any_ = pl.BlockSpec(memory_space=pl.ANY)
    vmem = pl.BlockSpec(memory_space=pltpu.VMEM)
    smem = pl.BlockSpec(memory_space=pltpu.SMEM)
    V = pltpu.VMEM
    dma = lambda *s: pltpu.SemaphoreType.DMA(s)
    np_ = 2 + 2 * NJ
    out = jax.ShapeDtypeStruct((ROWS, HQ), F32)
    gi, di, gt, dt = pl.pallas_call(
        kernel,
        out_shape=(out, out, out, out),
        in_specs=[any_] * 8 + [vmem, vmem, smem],
        out_specs=(vmem,) * 4,
        scratch_shapes=[
            V((RI, D), BF16), V((RT, D), BF16), V((RI, D), BF16), V((RT, D), BF16),
            V((4, CH, HB), BF16), V((NZ, 2 * RI, CH), BF16), V((NZ * 16, CH), BF16),
            V((RI + RT, CH), F32), V((SEQ, CH), F32),
            V((NZ, NX, 2 * RI, HQ), BF16), V((NX, 128, HQ), BF16),
            V((NZ, 3, 2 * RI, HQ), BF16), V((3, 128, HQ), BF16),
            V((NZ, NX, 2 * RI, HQ), BF16), V((NX, 128, HQ), BF16),
            V((SEQ, HQ), F32), V((NX, SEQ, HQ), F32), V((NX, SEQ, HQ), BF16),
            V((NZ, 64, CH), BF16), V((NZ, 16, CH), F32), V((NZ, 64, CH), BF16), V((NZ, 64, CH), BF16),
            V((SEQ, CH), F32), V((SEQ, CH), BF16),
            V((CH, SEQ), BF16), V((CH, SEQ), BF16), V((CH, 128), BF16), V((CH, 128), BF16),
            V((NJ, NX, SEQ, HJ), BF16), V((NJ, 3, SEQ, HJ), BF16), V((NJ, NX, SEQ, HJ), BF16),
            V((4, NX, CH, HQ), BF16), V((4, 2, CH, HQ), BF16), V((4, 3, ROWS, HQ), BF16),
            dma(4), dma(4), dma(4), dma(4), dma(4), dma(4), dma(4, 2), dma(4, 2),
            dma(NZ), dma(NZ), dma(NZ), dma(NZ),
            dma(9, 3), dma(9, 3), dma(9, 3), dma(9, 3), dma(NZ), dma(NZ), dma(NZ), dma(NZ), dma(NZ), dma(NZ),
            dma(NJ, 3), dma(NJ, 3), dma(NJ, 3), dma(NJ, 3), dma(np_, 2), dma(np_, 2), dma(np_, 3), dma(np_, 3),
        ],
        compiler_params=pltpu.CompilerParams(
            collective_id=0, has_side_effects=True, vmem_limit_bytes=60 * 1024 * 1024
        ),
    )(latent_image, latent_text, noise_image, noise_text, up_image, up_text, down_image, down_text, mod, coef, levels)
    return gi, di, gt, dt


def solution(mesh):
    placed = (
        P("dp", "col", None),
        P("dp", "col", None),
        P("dp", "col", None),
        P("dp", "col", None),
        P("row", "col"),
        P("row", "col"),
        P("row", "col"),
        P("row", "col"),
        P(),
        P("dp"),
        P("dp"),
        P("dp"),
    )
    grads = P("row", ("col", "dp"))
    return jax.shard_map(
        body, mesh=mesh, in_specs=placed, out_specs=(grads, grads, grads, grads), check_vma=False
    )
```

time: 769 us -> 208 us (0.27)
  waiting for transfers between devices: 556 us -> 0 us
  Pallas kernels: 0 us -> 193 us
  blocking collectives: 118 us -> 0 us
  local copies, waits for them, and re-layouts: 39.1 us -> 9.86 us
  matrix products: 24.3 us -> 0 us
  other arithmetic: 16.4 us -> 2.71 us
  between operations: 14.3 us -> 2.73 us
    unnamed x23 -> x0, waiting for transfers between devices: 420 us -> none
    pallas_call x0 -> x1, Pallas kernels: none -> 193 us  [body(): pl.pallas_call(kernel, out_shape=(out, out, out, out), in_specs=[any_] *...]
    all_gather x3 -> x0, waiting for transfers between devices: 135 us -> none  [the longest x2 96.1 us: gather_rows(): lax.all_gather(shortened(shares), 'row', axis=1, tiled=True)]
    all_gather x5 -> x0, blocking collectives: 118 us -> none  [the longest x2 58.8 us: gather_rows(): lax.all_gather(shortened(shares), 'row', axis=1, tiled=True)]
    unnamed x52 -> x10, local copies, waits for them, and re-layouts: 38.1 us -> 4.47 us
    dot_general x10 -> x0, matrix products: 24.3 us -> none  [the longest x4 9.78 us: share_rows(): jnp.einsum('std,df->stf', panel_rows, weight_rows, preferred_element_type...]
    convert_element_type x15 -> x0, other arithmetic: 8.11 us -> none  [the longest x4 3.43 us: body(): reduced = (lax.psum_scatter(gradients[0].astype(jnp.bfloat16), 'dp', scat...]
  transfers between devices with their start and end apart: 13 -> 0, of which waited for: 13 -> 0; matrix products, arithmetic and copies ran while one was open for 7% -> 0% of each run, Pallas kernels for 0% -> 0%
where the time goes in v1:
time: 208 us
  Pallas kernels  193 us (93%)
  local copies, waits for them, and re-layouts  9.86 us (5%)
  between operations  2.73 us (1%)
  other arithmetic  2.71 us (1%)
    pallas_call x1, Pallas kernels, body(): pl.pallas_call(kernel, out_shape=(out, out, out, out), in_specs=[any_] *...  193 us
    unnamed x10, local copies, waits for them, and re-layouts  4.47 us

profile of v1, /device:TPU:1, one launch (start us, length us, event | category | flops | bytes accessed | tf_op | source)
XLA Modules:
  0.0 208.1 jit_solution(16219890062855663187)
XLA Ops:
  0.7 1.2 dynamic_slice.16
  2.6 0.7 or_select_fusion
  3.3 1.2 dynamic_slice.15
  4.5 1.2 dynamic_slice.14
  7.0 1.2 broadcast_multiply_fusion
  8.3 0.2 fusion
  8.5 0.7 broadcast_in_dim.19.coef
  9.2 0.9 constant_dynamic-slice_fusion
  10.2 0.6 multiply_add_fusion.mod
  10.8 192.8 %shard_map.147 = (f32[384,384]{1,0:T(8,128)}, f32[384,384]{1,0:T(8,128)}, f32[384,384]{1,0:T(8,128)}, f32[384,384]{1,0:T(8,128)}) custom-call(bf16[2,56,3072]{2,1,0:T(8,128)(2,1)} %lat_i.1, bf16[2,8,3072]{2,1,0:T(8,128)(2,1)} %lat_t.1, bf16[2,56,3072]{2,1,0:T(8,128)(2,1)} %noi_i.1, bf16[2,8,3072]{2,1,0:T(8,128)(2,1)} %noi_t.1, bf16[384,1536]{1,0:T(8,128)(2,1)} %up_i.1, ...), custom_call_target="tpu_custom_call" | custom-call | tf_op jit(solution)/shard_map/pallas_call | solution.py:580
  203.6 0.0 copy-start.2
  203.6 0.0 copy-start.1
  203.6 2.0 copy.26
  205.7 0.0 copy-done.2
  205.7 0.0 copy-start
  205.7 0.8 copy.27
  206.5 0.0 copy-done.1
  206.5 0.8 copy.28
  207.3 0.0 copy-done
  207.3 0.8 copy.29
  (4 shorter events, 0.1 us)
Async XLA Ops:
  203.6 2.0 copy-start.2
  203.6 2.8 %copy-start.1 = (f32[384,384]{1,0:T(8,128)S(1)}, f32[384,384]{1,0:T(8,128)}, u32[]{:S(2)}) copy-start(f32[384,384]{1,0:T(8,128)} %get-tuple-element.16) | copy-start | bytes 1769476
  205.7 1.6 copy-start

commit v2 on v1

v2 whole, which is shorter than its diff:
```python
import functools
import math

import jax
import jax.numpy as jnp
from jax import lax
from jax.experimental import pallas as pl
from jax.experimental.pallas import tpu as pltpu
from jax.sharding import PartitionSpec as P

D = 3072
FF = 12288
IMG = 448
TXT = 64
STEPS = 1000
SEQ = 512
SAMPLES = 8

NX = 4
NZ = 8
CH = D // NX
HB = FF // NZ
HQ = HB // NX
RI = IMG // NZ
RT = TXT // NZ
NJ = 3
HJ = HQ // NJ
ROWS = D // 8
QR = ROWS // 4
NP = 3
PR = QR // NP
HR = ROWS // 2

GELU_SCALE = 0.7978845608028654
GELU_CUBIC = 0.044715
NORM_EPS = 1e-06
MESH = pl.DeviceIdType.MESH
F32 = jnp.float32
BF16 = jnp.bfloat16


def gelu_tanh(values):
    inner = GELU_SCALE * (values + GELU_CUBIC * values * values * values)
    return 0.5 * values * (1.0 + jnp.tanh(inner))


def gelu_slope(values):
    inner = GELU_SCALE * (values + GELU_CUBIC * values * values * values)
    tangent = jnp.tanh(inner)
    return 0.5 * (1.0 + tangent) + 0.5 * values * (1.0 - tangent * tangent) * GELU_SCALE * (
        1.0 + 3.0 * GELU_CUBIC * values * values
    )


def dot(a, b):
    return jnp.dot(a, b, preferred_element_type=F32)


def dot_nt(a, b):
    return lax.dot_general(a, b, (((1,), (1,)), ((), ())), preferred_element_type=F32)


class Sum:
    def __init__(self, part, relay, got, ss, rs, pos, to, s):
        self.part, self.relay, self.got, self.ss, self.rs, self.pos, self.to, self.s = part, relay, got, ss, rs, pos, to, s

    @property
    def relayed(self):
        return remote(self.part((self.pos + 2) % 4), self.relay, self.ss(0), self.rs(0), self.to(self.s))

    @property
    def direct(self):
        return remote(self.part((self.pos - self.s + 4) % 4), self.got(0), self.ss(1), self.rs(1), self.to(-self.s))

    @property
    def joined(self):
        return remote(self.part((self.pos + self.s + 4) % 4), self.got(1), self.ss(2), self.rs(2), self.to(self.s))

    def join(self):
        self.relayed.wait_recv()
        joint = self.part((self.pos + self.s + 4) % 4)
        joint[...] = (joint[...].astype(F32) + self.relay[...].astype(F32)).astype(BF16)
        self.joined.start()

    def first(self):
        self.relayed.start()
        self.direct.start()

    def wait(self):
        self.direct.wait_recv()
        self.joined.wait_recv()

    def sent(self):
        self.relayed.wait_send()
        self.direct.wait_send()
        self.joined.wait_send()


class Gather:
    def __init__(self, slot, ss, rs, pos, to, s):
        self.slot, self.ss, self.rs, self.pos, self.to, self.s = slot, ss, rs, pos, to, s

    @property
    def plus(self):
        return remote(self.slot(self.pos), self.slot(self.pos), self.ss(0), self.rs(0), self.to(self.s))

    @property
    def minus(self):
        return remote(self.slot(self.pos), self.slot(self.pos), self.ss(1), self.rs(1), self.to(-self.s))

    @property
    def onward(self):
        back = self.slot((self.pos - self.s + 4) % 4)
        return remote(back, back, self.ss(2), self.rs(2), self.to(self.s))

    def first(self):
        self.plus.start()
        self.minus.start()

    def forward(self):
        self.plus.wait_recv()
        self.onward.start()

    def wait(self):
        self.minus.wait_recv()
        self.onward.wait_recv()

    def sent(self):
        self.plus.wait_send()
        self.minus.wait_send()
        self.onward.wait_send()


def remote(src, dst, ss, rs, who):
    return pltpu.make_async_remote_copy(
        src_ref=src, dst_ref=dst, send_sem=ss, recv_sem=rs, device_id=who, device_id_type=MESH
    )


def kernel(
    lat_i, lat_t, noi_i, noi_t, up_i, up_t, dn_i, dn_t, modulation, feats, timesteps, skips, lengths,
    out_ui, out_di, out_ut, out_dt,
    lbi, lbt, nbi, nbt, W, uimg, utxt, ndiff, mod, coef, u32,
    stg, stgt, rrs, rrst, hid, hidt, pre_c, h32, hc,
    zst, rem, zr, errz, e32, ec, uT, eT, uTt, eTt, hgs, hgr, pg, G, CR, YR,
    s_loc, s_wl, s_w1s, s_w1r, s_w2s, s_w2r, s_w3s, s_w3r,
    s_zis, s_zir, s_zts, s_ztr,
    s_rss, s_rsr, s_ags, s_agr, s_mzs, s_mzr, s_mrs, s_mrr, s_ezs, s_ezr,
    s_hgs, s_hgr, s_pgs, s_pgr, s_cs, s_cr, s_ys, s_yr,
):
    r = lax.axis_index("row")
    z = lax.axis_index("col")
    d = lax.axis_index("dp")
    x, hi, lo, c = r // 2, r % 2, d // 2, d % 2
    y = hi * 2 + lo

    def dev(x, hi, lo, c, z):
        return (x * 2 + hi, z, lo * 2 + c)

    def xdev(t):
        return dev((x + t + NX) % NX, hi, lo, c, z)

    def zdev(t):
        return dev(x, hi, lo, c, (z + t + NZ) % NZ)

    def ydev(t):
        yy = (y + t + 4) % 4
        return dev(x, yy // 2, yy % 2, c, z)

    core = dev(x, hi, lo, 1 - c, z)
    adj = dev(x, 1 - hi, 1 - lo, c, z)
    side = dev(x, hi, 1 - lo, c, z)

    bar = pltpu.get_barrier_semaphore()
    for t in range(1, NX):
        pl.semaphore_signal(bar, inc=1, device_id=xdev(t), device_id_type=MESH)
    for t in range(1, NZ):
        pl.semaphore_signal(bar, inc=1, device_id=zdev(t), device_id_type=MESH)
    for t in range(1, 4):
        pl.semaphore_signal(bar, inc=1, device_id=ydev(t), device_id_type=MESH)
    pl.semaphore_signal(bar, inc=1, device_id=core, device_id_type=MESH)

    reads = [
        pltpu.make_async_copy(lat_i.at[hi], lbi, s_loc.at[0]),
        pltpu.make_async_copy(lat_t.at[hi], lbt, s_loc.at[1]),
        pltpu.make_async_copy(noi_i.at[hi], nbi, s_loc.at[2]),
        pltpu.make_async_copy(noi_t.at[hi], nbt, s_loc.at[3]),
    ]
    for cp in reads:
        cp.start()
    weights = (up_i, up_t, dn_i, dn_t)
    wl = [
        pltpu.make_async_copy(
            weights[m], W.at[m, pl.ds(pl.multiple_of(hi * ROWS, ROWS), ROWS)], s_wl.at[m]
        )
        for m in range(4)
    ]

    def wrows(m, half, quarter, p):
        return W.at[m, pl.ds(pl.multiple_of(half * ROWS + quarter * QR + p * PR, PR), PR)]

    q_mine = lo * 2 + c
    q_side = (1 - lo) * 2 + c

    def w1(m, p):
        return remote(
            weights[m].at[pl.ds(pl.multiple_of(q_side * QR + p * PR, PR), PR)],
            wrows(m, hi, q_side, p), s_w1s.at[m, p], s_w1r.at[m, p], adj,
        )

    def w1in(m, p):
        rows = wrows(m, 1 - hi, q_mine, p)
        return remote(rows, rows, s_w1s.at[m, p], s_w1r.at[m, p], adj)

    def w2(m, p):
        rows = wrows(m, 1 - hi, q_mine, p)
        return remote(rows, rows, s_w2s.at[m, p], s_w2r.at[m, p], side)

    def w2in(m, p):
        rows = wrows(m, 1 - hi, q_side, p)
        return remote(rows, rows, s_w2s.at[m, p], s_w2r.at[m, p], side)

    def w3(m, p, k):
        rows = wrows(m, 1 - hi, q_side if k else q_mine, p)
        return remote(rows, rows, s_w3s.at[m, p, k], s_w3r.at[m, p, k], core)

    def w_step1(m):
        for p in range(NP):
            w1in(m, p).wait_recv()
            w2(m, p).start()
            w3(m, p, 0).start()

    def w_step2(m):
        for p in range(NP):
            w2in(m, p).wait_recv()
            w3(m, p, 1).start()

    def w_step3(m):
        wl[m].wait()
        for p in range(NP):
            w3(m, p, 0).wait_recv()
            w3(m, p, 1).wait_recv()

    for cp in wl:
        cp.start()
    lane0 = pl.multiple_of(x * CH, CH)
    own_lanes = pl.ds(lane0, CH)
    for k in range(2):
        for a in range(3):
            for b in range(2):
                mod[k, a, b : b + 1, :] = (
                    modulation[k, a, 0:1, own_lanes] + modulation[k, a, 1:2, own_lanes] * feats[b * 2 + hi, :, own_lanes]
                )
    t_s = timesteps[hi]
    t_g = t_s - skips[hi]
    levels = (t_s.astype(F32) * (1.0 / STEPS), t_g.astype(F32) * (1.0 / STEPS))
    length = lengths[hi]
    row = lax.broadcasted_iota(jnp.int32, (RI + RT, 128), 0)
    valid = jnp.logical_or(row < RI, row + (z * RT - RI) < length)
    count = jnp.full((RI + RT, 128), IMG, F32) + length.astype(F32)
    coef[...] = jnp.where(valid, SEQ / math.sqrt(SAMPLES * SEQ) / count, 0.0)
    for cp in reads:
        cp.wait()
    for latb, noib, rows, stream, base in ((lbi, nbi, RI, 0, 0), (lbt, nbt, RT, 1, RI)):
        lat_own = latb[:, own_lanes].astype(F32)
        noi_own = noib[:, own_lanes].astype(F32)
        owns = []
        us = []
        for b in range(2):
            level = levels[b]
            full = (1.0 - level) * latb[...].astype(F32) + level * noib[...].astype(F32)
            mean = jnp.mean(full, axis=-1, keepdims=True)
            cen = full - mean
            var = jnp.mean(cen * cen, axis=-1, keepdims=True)
            own = (1.0 - level) * lat_own + level * noi_own
            owns.append(own)
            normed = (own - mean) * lax.rsqrt(var + NORM_EPS)
            us.append(normed * (1.0 + mod[stream, 1, b : b + 1, :]) + mod[stream, 0, b : b + 1, :])
        ndiff[base : base + rows, :] = owns[0] - owns[1]
        both = jnp.concatenate(us, axis=0).astype(BF16)
        if stream == 0:
            uimg[0] = both
        else:
            utxt[0:16, :] = both

    pl.semaphore_wait(bar, 14)
    for m in range(4):
        for p in range(NP):
            w1(m, p).start()

    def send_z(i, to, who):
        a = remote(uimg.at[i], uimg.at[to], s_zis.at[to], s_zir.at[to], who)
        b = remote(
            utxt.at[pl.ds(pl.multiple_of(i * 16, 16), 16)],
            utxt.at[pl.ds(pl.multiple_of(to * 16, 16), 16)],
            s_zts.at[to], s_ztr.at[to], who,
        )
        return a, b

    for to, who in ((1, zdev(1)), (2, zdev(-1))):
        for cp in send_z(0, to, who):
            cp.start()

    w_step1(0)
    w_step2(0)
    w_step3(0)

    def sign(i):
        return 1 - 2 * (i % 2)

    def rs_img(i):
        return Sum(
            lambda q: stg.at[i, q], rrs.at[i, 2], lambda k: rrs.at[i, k],
            lambda k: s_rss.at[i, k], lambda k: s_rsr.at[i, k], x, xdev, sign(i),
        )

    def ag_img(i):
        return Gather(lambda q: hid.at[i, q], lambda k: s_ags.at[i, k], lambda k: s_agr.at[i, k], x, xdev, sign(i))

    def rs_txt(h):
        rows = pl.ds(h * 64, 64)
        return Sum(
            lambda q: stgt.at[q, rows], rrst.at[2, rows], lambda k: rrst.at[k, rows],
            lambda k: s_rss.at[8 + h, k], lambda k: s_rsr.at[8 + h, k], x, xdev, 1 - 2 * h,
        )

    def ag_txt(h):
        rows = pl.ds(h * 64, 64)
        return Gather(
            lambda q: hidt.at[q, rows], lambda k: s_ags.at[8 + h, k], lambda k: s_agr.at[8 + h, k], x, xdev, 1 - 2 * h
        )

    def up_chunk(i):
        @pl.when(i > 0)
        def _():
            a, b = send_z(i, i, zdev(1))
            a.wait_recv()
            b.wait_recv()

        @pl.when(jnp.logical_and(i > 0, i < 6))
        def _():
            for cp in send_z(i, i + 2, zdev((i % 2) * 2 - 1)):
                cp.start()

        u = uimg[i]
        for q in range(NX):
            stg[i, q] = dot(u, W[0, :, q * HQ : (q + 1) * HQ]).astype(BF16)
        rs_img(i).first()

    def at(k, step, do, *args):
        @pl.when(k == step)
        def _():
            do(*args)

    def up_step(k, _):
        @pl.when(k < NZ)
        def _():
            up_chunk(k)

        @pl.when(k >= 2)
        def _():
            rs_img(k - 2).join()

        at(k, 1, w_step1, 1)
        at(k, 3, w_step1, 2)
        at(k, 4, w_step2, 1)
        at(k, 6, w_step1, 3)
        at(k, 7, w_step2, 2)
        return 0

    lax.fori_loop(0, NZ + 2, up_step, 0)

    w_step3(1)
    for q in range(NX):
        stgt[q] = dot(utxt[...], W[1, :, q * HQ : (q + 1) * HQ]).astype(BF16)
    for h in range(2):
        rs_txt(h).first()
    w_step2(3)

    def pack_u(i, _):
        u32[pl.ds(pl.multiple_of(i * RI, 8), RI), :] = uimg[i].astype(F32)[0:RI]
        u32[pl.ds(pl.multiple_of(IMG + i * RT, 8), RT), :] = utxt[
            pl.ds(pl.multiple_of(i * 16, 16), 16), :
        ].astype(F32)[0:RT]
        return 0

    lax.fori_loop(0, NZ, pack_u, 0)

    def act_chunk(i):
        rs_img(i).wait()
        pre = stg[i, x].astype(F32) + rrs[i, 0].astype(F32) + rrs[i, 1].astype(F32)
        pre_c[pl.ds(pl.multiple_of(i * RI, 8), RI), :] = pre[0:RI]
        hid[i, x] = gelu_tanh(pre).astype(BF16)
        ag_img(i).first()

    def join_text():
        for h in range(2):
            rs_txt(h).join()

    def act_text():
        for h in range(2):
            rs_txt(h).wait()
        pre = stgt[x].astype(F32) + rrst[0].astype(F32) + rrst[1].astype(F32)
        for i in range(NZ):
            pre_c[IMG + i * RT : IMG + (i + 1) * RT, :] = pre[i * 16 : i * 16 + RT]
        hidt[x] = gelu_tanh(pre).astype(BF16)
        for h in range(2):
            ag_txt(h).first()

    def pass_text():
        for h in range(2):
            ag_txt(h).forward()

    def zslot(i):
        half = (i + 1) // 2
        return (NZ + half - 2 * half * (i % 2)) % NZ

    def mz_main(i):
        s = zslot(i)
        return remote(zst.at[i, 0:48], zr.at[s, 0:48], s_mzs.at[i], s_mzr.at[s], zdev(s))

    def mz_rest(i):
        s = zslot(i)
        return remote(zst.at[i, 48:64], zr.at[s, 48:64], s_mrs.at[i], s_mrr.at[s], zdev(s))

    def down_chunk(i):
        ag_img(i).wait()
        out = dot_nt(hid[i, 0], W[2, :, 0:HQ])
        for q in range(1, NX):
            out = out + dot_nt(hid[i, q], W[2, :, q * HQ : (q + 1) * HQ])
        diff = mod[0, 2, 0:1, :] * out[0:RI] - mod[0, 2, 1:2, :] * out[RI : 2 * RI]
        zst[i, 0:48, :] = diff[0:48].astype(BF16)
        rem[i, 0:8, :] = diff[48:56]

        @pl.when(i > 0)
        def _():
            mz_main(i).start()

        for q in range(NX):
            h32[q, pl.ds(pl.multiple_of(i * RI, 8), RI), :] = hid[i, q].astype(F32)[0:RI]

    def rest_chunk(i, _):
        zst[i, 48:64, :] = rem[i].astype(BF16)

        @pl.when(i > 0)
        def _():
            mz_rest(i).start()

        return 0

    def down_text():
        for h in range(2):
            ag_txt(h).wait()
        out = dot_nt(hidt[0], W[3, :, 0:HQ])
        for q in range(1, NX):
            out = out + dot_nt(hidt[q], W[3, :, q * HQ : (q + 1) * HQ])
        for i in range(NZ):
            rem[i, 8:16, :] = (
                mod[1, 2, 0:1, :] * out[i * 16 : i * 16 + RT] - mod[1, 2, 1:2, :] * out[i * 16 + RT : (i + 1) * 16]
            )
        for q in range(NX):
            full = hidt[q].astype(F32)
            for i in range(NZ):
                h32[q, IMG + i * RT : IMG + (i + 1) * RT, :] = full[i * 16 : i * 16 + RT]

    def down_rest():
        w_step3(3)
        down_text()
        lax.fori_loop(3, NZ, rest_chunk, 0)

    def order(k):
        return k + 3 + (k // 5) * (4 - 2 * k)

    def hidden_step(k, _):
        @pl.when(k < NZ)
        def _():
            act_chunk(order(k))

        at(k, 2, join_text)
        at(k, 4, act_text)

        @pl.when(jnp.logical_and(k >= 1, k <= NZ))
        def _():
            ag_img(order(k - 1)).forward()

        at(k, 6, pass_text)
        at(k, 3, w_step3, 2)

        @pl.when(k >= 3)
        def _():
            down_chunk(order(k - 3))

        at(k, 7, down_rest)

        @pl.when(k >= 8)
        def _():
            rest_chunk(order(k - 3), 0)

        return 0

    lax.fori_loop(0, NZ + 3, hidden_step, 0)

    img_lane = lax.broadcasted_iota(jnp.int32, (CH, SEQ), 1) < IMG
    txt_lane = lax.broadcasted_iota(jnp.int32, (CH, 128), 1) >= 64
    turned = u32[...].T
    uT[...] = jnp.where(img_lane, turned, 0.0).astype(BF16)
    uTt[...] = jnp.where(txt_lane, turned[:, SEQ - 128 :], 0.0).astype(BF16)
    hc[...] = h32[...].astype(BF16)

    total = ndiff[...] + zst[0].astype(F32)
    for s in range(1, NZ):
        a = remote(zst.at[s, 0:48], zr.at[s, 0:48], s_mzs.at[s], s_mzr.at[s], zdev(s))
        b = remote(zst.at[s, 48:64], zr.at[s, 48:64], s_mrs.at[s], s_mrr.at[s], zdev(s))
        a.wait_recv()
        b.wait_recv()
        total = total + zr[s].astype(F32)
    total = total * coef[:, 0:1]
    err_i = mod[0, 2, 0:1, :] * total[0:RI]
    err_t = mod[1, 2, 0:1, :] * total[RI : RI + RT]
    errz[0] = jnp.concatenate([err_i, err_t], axis=0).astype(BF16)

    def send_e(i, to, who):
        return remote(errz.at[i], errz.at[to], s_ezs.at[to], s_ezr.at[to], who)

    send_e(0, 1, zdev(1)).start()
    send_e(0, 2, zdev(-1)).start()

    def err_chunk(i, _):
        @pl.when(i > 0)
        def _():
            send_e(i, i, zdev(1)).wait_recv()

        @pl.when(jnp.logical_and(i > 0, i < 6))
        def _():
            send_e(i, i + 2, zdev((i % 2) * 2 - 1)).start()

        full = errz[i].astype(F32)
        e32[pl.ds(pl.multiple_of(i * RI, 8), RI), :] = full[0:RI]
        e32[pl.ds(pl.multiple_of(IMG + i * RT, 8), RT), :] = full[RI : RI + RT]
        return 0

    lax.fori_loop(0, NZ, err_chunk, 0)
    ec[...] = e32[...].astype(BF16)

    def hg_block(q, _):
        lanes = pl.ds(pl.multiple_of(q * HQ, HQ), HQ)
        gi = dot(ec[0:IMG], W[2, :, lanes]).astype(BF16)
        gt = dot(ec[IMG:SEQ], W[3, :, lanes]).astype(BF16)
        for j in range(NJ):
            hgs[j, q, 0:IMG, :] = gi[:, j * HJ : (j + 1) * HJ]
            hgs[j, q, IMG:SEQ, :] = gt[:, j * HJ : (j + 1) * HJ]
        return 0

    lax.fori_loop(0, NX, hg_block, 0)

    def rs_hg(j, h):
        rows = pl.ds(h * 256, 256)
        return Sum(
            lambda q: hgs.at[j, q, rows], hgr.at[j, 2, rows], lambda k: hgr.at[j, k, rows],
            lambda k: s_hgs.at[j, h, k], lambda k: s_hgr.at[j, h, k], x, xdev, 1 - 2 * h,
        )

    def ag_pg(j, h):
        rows = pl.ds(h * 256, 256)
        return Gather(
            lambda q: pg.at[j, q, rows], lambda k: s_pgs.at[j, h, k], lambda k: s_pgr.at[j, h, k], x, xdev, 1 - 2 * h
        )

    units = [(j, h) for j in range(NJ) for h in range(2)]
    for j, h in units:
        rs_hg(j, h).relayed.start()
    for j, h in units:
        rs_hg(j, h).direct.start()

    turned = e32[...].T
    eT[...] = jnp.where(img_lane, turned, 0.0).astype(BF16)
    eTt[...] = jnp.where(txt_lane, turned[:, SEQ - 128 :], 0.0).astype(BF16)

    def gd_block(q, _):
        G[0, q] = dot(eT[...], hc[q]).astype(BF16)
        G[1, q] = dot(eTt[...], hc[q, SEQ - 128 :, :]).astype(BF16)
        return 0

    lax.fori_loop(0, NX, gd_block, 0)

    def cols(m, j):
        return pl.ds(0, HQ) if j is None else pl.ds(j * HJ, HJ)

    def core_cp(p, m, j, l):
        return remote(
            G.at[m, l * 2 + 1 - c, :, cols(m, j)], CR.at[m, l, :, cols(m, j)], s_cs.at[p, l], s_cr.at[p, l], core
        )

    def rs_y(p, m, j, h):
        rows = pl.ds(h * HR, HR)
        return Sum(
            lambda yy: G.at[
                m, (yy % 2) * 2 + c, pl.ds(pl.multiple_of((yy // 2) * ROWS + h * HR, HR), HR), cols(m, j)
            ],
            YR.at[m, 2, rows, cols(m, j)], lambda k: YR.at[m, k, rows, cols(m, j)],
            lambda k: s_ys.at[p, h, k], lambda k: s_yr.at[p, h, k], y, ydev, 1 - 2 * h,
        )

    def join_y(p, m, j):
        for h in range(2):
            rs_y(p, m, j, h).join()

    def after_core(p, m, j):
        for l in range(2):
            core_cp(p, m, j, l).wait_recv()
            G[m, l * 2 + c, :, cols(m, j)] = (
                G[m, l * 2 + c, :, cols(m, j)].astype(F32) + CR[m, l, :, cols(m, j)].astype(F32)
            ).astype(BF16)
        for h in range(2):
            rs_y(p, m, j, h).relayed.start()
        for h in range(2):
            rs_y(p, m, j, h).direct.start()

    for m in range(2):
        for l in range(2):
            core_cp(m, m, None, l).start()

    def pre_grad(j):
        for h in range(2):
            rs_hg(j, h).wait()
        g = hgs[j, x].astype(F32) + hgr[j, 0].astype(F32) + hgr[j, 1].astype(F32)
        pg[j, x] = (g * gelu_slope(pre_c[:, j * HJ : (j + 1) * HJ])).astype(BF16)
        for h in range(2):
            ag_pg(j, h).first()

    def pass_pg(j):
        for h in range(2):
            ag_pg(j, h).forward()

    for j, h in units:
        rs_hg(j, h).join()
    after_core(0, 0, None)
    after_core(1, 1, None)
    pre_grad(0)
    pre_grad(1)
    pass_pg(0)
    join_y(0, 0, None)
    pre_grad(2)
    pass_pg(1)
    join_y(1, 1, None)
    pass_pg(2)

    for j in range(NJ):
        for h in range(2):
            ag_pg(j, h).wait()
        wide = jnp.concatenate([pg[j, q] for q in range(NX)], axis=1)
        gi = dot(uT[...], wide).astype(BF16)
        gt = dot(uTt[...], wide[SEQ - 128 :]).astype(BF16)
        for q in range(NX):
            G[2, q, :, j * HJ : (j + 1) * HJ] = gi[:, q * HJ : (q + 1) * HJ]
            G[3, q, :, j * HJ : (j + 1) * HJ] = gt[:, q * HJ : (q + 1) * HJ]
        for k in range(2):
            for l in range(2):
                core_cp(2 + 2 * j + k, 2 + k, j, l).start()
        for k in range(2):
            after_core(2 + 2 * j + k, 2 + k, j)
        if j > 0:
            for k in range(2):
                join_y(2 * j + k, 2 + k, j - 1)
    for k in range(2):
        join_y(2 * NJ + k, 2 + k, NJ - 1)

    mine = pl.ds(pl.multiple_of(hi * ROWS, ROWS), ROWS)

    def finish(p, m, j, out):
        for h in range(2):
            rs_y(p, m, j, h).wait()
        g = G[m, lo * 2 + c, mine, cols(m, j)].astype(F32)
        for k in range(2):
            g = g + YR[m, k, :, cols(m, j)].astype(F32)
        out[:, cols(m, j)] = g

    finish(0, 0, None, out_di)
    finish(1, 1, None, out_dt)
    for j in range(NJ):
        finish(2 + 2 * j, 2, j, out_ui)
        finish(3 + 2 * j, 3, j, out_ut)

    for m in range(4):
        for p in range(NP):
            w1(m, p).wait_send()
            w2(m, p).wait_send()
            w3(m, p, 0).wait_send()
            w3(m, p, 1).wait_send()

    def sent(i, _):
        @pl.when(i > 0)
        def _():
            a, b = send_z(i, i, zdev(1))
            a.wait_send()
            b.wait_send()
            send_e(i, i, zdev(1)).wait_send()
            mz_main(i).wait_send()
            mz_rest(i).wait_send()

        rs_img(i).sent()
        ag_img(i).sent()
        return 0

    lax.fori_loop(0, NZ, sent, 0)
    for h in range(2):
        rs_txt(h).sent()
        ag_txt(h).sent()
    for j, h in units:
        rs_hg(j, h).sent()
        ag_pg(j, h).sent()
    parts = [(0, 0, None), (1, 1, None)] + [(2 + 2 * j + k, 2 + k, j) for j in range(NJ) for k in range(2)]
    for p, m, j in parts:
        for l in range(2):
            core_cp(p, m, j, l).wait_send()
        for h in range(2):
            rs_y(p, m, j, h).sent()


def widen(a, b, c, d, oa, ob, oc, od):
    for src, dst in ((a, oa), (b, ob), (c, oc), (d, od)):
        dst[...] = src[...]


def body(
    latent_image, latent_text, noise_image, noise_text, up_image, down_image, up_text, down_text,
    modulation, timesteps, skips, text_lengths,
):
    half = D // 2
    frequency = jnp.exp(-math.log(10000.0) * jnp.arange(half).astype(F32) / half)
    times = jnp.concatenate([timesteps, timesteps - skips]).astype(F32)
    angles = times[:, None] * frequency[None, :]
    feats = jnp.concatenate([jnp.cos(angles), jnp.sin(angles)], axis=1)[:, None, :]

    any_ = pl.BlockSpec(memory_space=pl.ANY)
    vmem = pl.BlockSpec(memory_space=pltpu.VMEM)
    smem = pl.BlockSpec(memory_space=pltpu.SMEM)
    V = pltpu.VMEM
    dma = lambda *s: pltpu.SemaphoreType.DMA(s)
    parts = 2 + 2 * NJ
    out = jax.ShapeDtypeStruct((ROWS, HQ), F32)
    grads = pl.pallas_call(
        kernel,
        out_shape=(out, out, out, out),
        in_specs=[any_] * 8 + [vmem, vmem, smem, smem, smem],
        out_specs=(vmem,) * 4,
        scratch_shapes=[
            V((RI, D), BF16), V((RT, D), BF16), V((RI, D), BF16), V((RT, D), BF16),
            V((4, CH, HB), BF16), V((NZ, 2 * RI, CH), BF16), V((NZ * 16, CH), BF16),
            V((RI + RT, CH), F32), V((2, 3, 2, CH), F32), V((RI + RT, 128), F32), V((SEQ, CH), F32),
            V((NZ, NX, 2 * RI, HQ), BF16), V((NX, 128, HQ), BF16),
            V((NZ, 3, 2 * RI, HQ), BF16), V((3, 128, HQ), BF16),
            V((NZ, NX, 2 * RI, HQ), BF16), V((NX, 128, HQ), BF16),
            V((SEQ, HQ), F32), V((NX, SEQ, HQ), F32), V((NX, SEQ, HQ), BF16),
            V((NZ, 64, CH), BF16), V((NZ, 16, CH), F32), V((NZ, 64, CH), BF16), V((NZ, 64, CH), BF16),
            V((SEQ, CH), F32), V((SEQ, CH), BF16),
            V((CH, SEQ), BF16), V((CH, SEQ), BF16), V((CH, 128), BF16), V((CH, 128), BF16),
            V((NJ, NX, SEQ, HJ), BF16), V((NJ, 3, SEQ, HJ), BF16), V((NJ, NX, SEQ, HJ), BF16),
            V((4, NX, CH, HQ), BF16), V((4, 2, CH, HQ), BF16), V((4, 3, ROWS, HQ), BF16),
            dma(4), dma(4), dma(4, NP), dma(4, NP), dma(4, NP), dma(4, NP), dma(4, NP, 2), dma(4, NP, 2),
            dma(NZ), dma(NZ), dma(NZ), dma(NZ),
            dma(10, 3), dma(10, 3), dma(10, 3), dma(10, 3), dma(NZ), dma(NZ), dma(NZ), dma(NZ), dma(NZ), dma(NZ),
            dma(NJ, 2, 3), dma(NJ, 2, 3), dma(NJ, 2, 3), dma(NJ, 2, 3), dma(parts, 2), dma(parts, 2), dma(parts, 2, 3), dma(parts, 2, 3),
        ],
        compiler_params=pltpu.CompilerParams(
            collective_id=0, has_side_effects=True, vmem_limit_bytes=60 * 1024 * 1024
        ),
    )(
        latent_image, latent_text, noise_image, noise_text, up_image, up_text, down_image, down_text,
        modulation, feats, timesteps, skips, text_lengths,
    )
    return pl.pallas_call(
        widen, out_shape=(out, out, out, out), in_specs=[vmem] * 4, out_specs=(vmem,) * 4,
    )(*grads)


def solution(mesh):
    placed = (
        P("dp", "col", None),
        P("dp", "col", None),
        P("dp", "col", None),
        P("dp", "col", None),
        P("row", "col"),
        P("row", "col"),
        P("row", "col"),
        P("row", "col"),
        P(),
        P("dp"),
        P("dp"),
        P("dp"),
    )
    grads = P("row", ("col", "dp"))
    return jax.shard_map(
        body, mesh=mesh, in_specs=placed, out_specs=(grads, grads, grads, grads), check_vma=False
    )
```

time: 208 us -> 166 us (0.80)
  Pallas kernels: 193 us -> 163 us
  local copies, waits for them, and re-layouts: 9.86 us -> 0.65 us
  between operations: 2.73 us -> 0.65 us
    pallas_call x1, Pallas kernels: 193 us -> 160 us  [body(): pl.pallas_call(kernel, out_shape=(out, out, out, out), in_specs=[any_] *...]
    unnamed x10 -> x0, local copies, waits for them, and re-layouts: 4.47 us -> none
    dynamic_slice x3 -> x0, local copies, waits for them, and re-layouts: 3.72 us -> none  [the longest x1 1.24 us: body(): t_g = t_s - lax.dynamic_index_in_dim(skips, hi, 0, False)]
    pallas_call x0 -> x1, Pallas kernels: none -> 3.04 us  [body(): pl.pallas_call(widen, out_shape=(out, out, out, out), in_specs=[vmem] * 4...]
where the time goes in v2:
time: 166 us
  Pallas kernels  163 us (98%)
  other arithmetic  1.68 us (1%)
    pallas_call x1, Pallas kernels, body(): pl.pallas_call(kernel, out_shape=(out, out, out, out), in_specs=[any_] *...  160 us

profile of v2, /device:TPU:1, one launch (start us, length us, event | category | flops | bytes accessed | tf_op | source)
XLA Modules:
  0.0 165.7 jit_solution(8070482485848921564)
XLA Ops:
  0.6 0.7 sub.3
  1.3 0.7 add_convert_fusion
  2.0 0.3 multiply_cosine_fusion
  2.3 0.7 broadcast_in_dim.2.feats
  3.0 159.6 %shard_map.147 = (f32[384,384]{1,0:T(8,128)}, f32[384,384]{1,0:T(8,128)}, f32[384,384]{1,0:T(8,128)}, f32[384,384]{1,0:T(8,128)}) custom-call(bf16[2,56,3072]{2,1,0:T(8,128)(2,1)} %lat_i.1, bf16[2,8,3072]{2,1,0:T(8,128)(2,1)} %lat_t.1, bf16[2,56,3072]{2,1,0:T(8,128)(2,1)} %noi_i.1, bf16[2,8,3072]{2,1,0:T(8,128)(2,1)} %noi_t.1, bf16[384,1536]{1,0:T(8,128)(2,1)} %up_i.1, ...), custom_call_target="tpu_custom_call" | custom-call | tf_op jit(solution)/shard_map/pallas_call | solution.py:742
  162.6 3.0 %shard_map.148 = (f32[384,384]{1,0:T(8,128)}, f32[384,384]{1,0:T(8,128)}, f32[384,384]{1,0:T(8,128)}, f32[384,384]{1,0:T(8,128)}) custom-call(f32[384,384]{1,0:T(8,128)} %get-tuple-element.8.a, f32[384,384]{1,0:T(8,128)} %get-tuple-element.9.b, f32[384,384]{1,0:T(8,128)} %get-tuple-element.10.c, f32[384,384]{1,0:T(8,128)} %get-tuple-element.11.d), custom_call_target="tpu_custom_call" | custom-call | tf_op jit(solution)/shard_map/pallas_call | solution.py:772
  (2 shorter events, 0.0 us)

commit v3 on v2

--- a/solution.py
+++ b/solution.py
@@ -23,6 +23,7 @@
 HQ = HB // NX
 RI = IMG // NZ
 RT = TXT // NZ
+RC = RI + RT
 NJ = 3
 HJ = HQ // NJ
 ROWS = D // 8
@@ -142,11 +143,11 @@
     out_ui, out_di, out_ut, out_dt,
     lbi, lbt, nbi, nbt, W, uimg, utxt, ndiff, mod, coef, u32,
     stg, stgt, rrs, rrst, hid, hidt, pre_c, h32, hc,
-    zst, rem, zr, errz, e32, ec, uT, eT, uTt, eTt, hgs, hgr, pg, G, CR, YR,
+    zst, rem, zr, errz, t32, uT, eT, hgs, hgr, pg, G, CR, YR, TS, TA, OB,
     s_loc, s_wl, s_w1s, s_w1r, s_w2s, s_w2r, s_w3s, s_w3r,
     s_zis, s_zir, s_zts, s_ztr,
     s_rss, s_rsr, s_ags, s_agr, s_mzs, s_mzr, s_mrs, s_mrr, s_ezs, s_ezr,
-    s_hgs, s_hgr, s_pgs, s_pgr, s_cs, s_cr, s_ys, s_yr,
+    s_hgs, s_hgr, s_pgs, s_pgr, s_cs, s_cr, s_ys, s_yr, s_ts, s_tr, s_out,
 ):
     r = lax.axis_index("row")
     z = lax.axis_index("col")
@@ -167,6 +168,10 @@
         yy = (y + t + 4) % 4
         return dev(x, yy // 2, yy % 2, c, z)
 
+    def tdev(t, k):
+        yy = (y + t) % 4
+        return dev(x, yy // 2, yy % 2, c + k - 2 * c * k, z)
+
     core = dev(x, hi, lo, 1 - c, z)
     adj = dev(x, 1 - hi, 1 - lo, c, z)
     side = dev(x, hi, 1 - lo, c, z)
@@ -176,9 +181,9 @@
         pl.semaphore_signal(bar, inc=1, device_id=xdev(t), device_id_type=MESH)
     for t in range(1, NZ):
         pl.semaphore_signal(bar, inc=1, device_id=zdev(t), device_id_type=MESH)
-    for t in range(1, 4):
-        pl.semaphore_signal(bar, inc=1, device_id=ydev(t), device_id_type=MESH)
-    pl.semaphore_signal(bar, inc=1, device_id=core, device_id_type=MESH)
+    others = [(t, k) for t in range(4) for k in range(2) if t or k]
+    for t, k in others:
+        pl.semaphore_signal(bar, inc=1, device_id=tdev(t, k), device_id_type=MESH)
 
     reads = [
         pltpu.make_async_copy(lat_i.at[hi], lbi, s_loc.at[0]),
@@ -283,10 +288,9 @@
         else:
             utxt[0:16, :] = both
 
-    pl.semaphore_wait(bar, 14)
-    for m in range(4):
-        for p in range(NP):
-            w1(m, p).start()
+    pl.semaphore_wait(bar, 17)
+    for p in range(NP):
+        w1(0, p).start()
 
     def send_z(i, to, who):
         a = remote(uimg.at[i], uimg.at[to], s_zis.at[to], s_zir.at[to], who)
@@ -301,7 +305,20 @@
         for cp in send_z(0, to, who):
             cp.start()
 
+    def z_pass(i):
+        a, b = send_z(i, i, zdev(1))
+        a.wait_recv()
+        b.wait_recv()
+        if i < 6:
+            for cp in send_z(i, i + 2, zdev((i % 2) * 2 - 1)):
+                cp.start()
+
     w_step1(0)
+    for m in range(1, 4):
+        for p in range(NP):
+            w1(m, p).start()
+    z_pass(1)
+    z_pass(2)
     w_step2(0)
     w_step3(0)
 
@@ -331,13 +348,13 @@
         )
 
     def up_chunk(i):
-        @pl.when(i > 0)
+        @pl.when(i > 2)
         def _():
             a, b = send_z(i, i, zdev(1))
             a.wait_recv()
             b.wait_recv()
 
-        @pl.when(jnp.logical_and(i > 0, i < 6))
+        @pl.when(jnp.logical_and(i > 2, i < 6))
         def _():
             for cp in send_z(i, i + 2, zdev((i % 2) * 2 - 1)):
                 cp.start()
@@ -378,18 +395,43 @@
     w_step2(3)
 
     def pack_u(i, _):
-        u32[pl.ds(pl.multiple_of(i * RI, 8), RI), :] = uimg[i].astype(F32)[0:RI]
-        u32[pl.ds(pl.multiple_of(IMG + i * RT, 8), RT), :] = utxt[
-            pl.ds(pl.multiple_of(i * 16, 16), 16), :
-        ].astype(F32)[0:RT]
+        u32[pl.ds(pl.multiple_of(i * RC, 8), RI), :] = uimg[i].astype(F32)[0:RI]
+        text = utxt[pl.ds(pl.multiple_of(i * 16, 16), 16), :].astype(F32)[0:RT]
+        u32[pl.ds(pl.multiple_of(i * RC + RI, 8), RT), :] = text
+        t32[pl.ds(pl.multiple_of(i * RT, 8), RT), :] = text
         return 0
 
     lax.fori_loop(0, NZ, pack_u, 0)
+
+    def text_cp(f, t, k):
+        yy = (y + t) % 4
+        src = TS.at[f, yy // 2] if f % 2 == 0 else TS.at[f, (yy % 2) * 2 + c + k - 2 * c * k]
+        return remote(src, TA.at[f, k, t], s_ts.at[f, t, k], s_tr.at[f, t, k], tdev(t, k))
+
+    def send_text(f):
+        TA[f, 0, 0] = TS[f, hi] if f % 2 == 0 else TS[f, q_mine]
+        for t, k in others:
+            text_cp(f, t, k).start()
+
+    def wait_text(f):
+        for t, k in others:
+            text_cp(f, t, k).wait_recv()
+
+    def sent_text(f):
+        for t, k in others:
+            text_cp(f, t, k).wait_send()
+
+    def halves(f):
+        for h in range(2):
+            TS[f, h] = t32[:, h * ROWS : (h + 1) * ROWS].astype(BF16)
+
+    halves(0)
+    send_text(0)
 
     def act_chunk(i):
         rs_img(i).wait()
         pre = stg[i, x].astype(F32) + rrs[i, 0].astype(F32) + rrs[i, 1].astype(F32)
-        pre_c[pl.ds(pl.multiple_of(i * RI, 8), RI), :] = pre[0:RI]
+        pre_c[pl.ds(pl.multiple_of(i * RC, 8), RI), :] = pre[0:RI]
         hid[i, x] = gelu_tanh(pre).astype(BF16)
         ag_img(i).first()
 
@@ -402,7 +444,7 @@
             rs_txt(h).wait()
         pre = stgt[x].astype(F32) + rrst[0].astype(F32) + rrst[1].astype(F32)
         for i in range(NZ):
-            pre_c[IMG + i * RT : IMG + (i + 1) * RT, :] = pre[i * 16 : i * 16 + RT]
+            pre_c[i * RC + RI : (i + 1) * RC, :] = pre[i * 16 : i * 16 + RT]
         hidt[x] = gelu_tanh(pre).astype(BF16)
         for h in range(2):
             ag_txt(h).first()
@@ -437,7 +479,7 @@
             mz_main(i).start()
 
         for q in range(NX):
-            h32[q, pl.ds(pl.multiple_of(i * RI, 8), RI), :] = hid[i, q].astype(F32)[0:RI]
+            h32[q, pl.ds(pl.multiple_of(i * RC, 8), RI), :] = hid[i, q].astype(F32)[0:RI]
 
     def rest_chunk(i, _):
         zst[i, 48:64, :] = rem[i].astype(BF16)
@@ -460,8 +502,11 @@
             )
         for q in range(NX):
             full = hidt[q].astype(F32)
+            text = [full[i * 16 : i * 16 + RT] for i in range(NZ)]
             for i in range(NZ):
-                h32[q, IMG + i * RT : IMG + (i + 1) * RT, :] = full[i * 16 : i * 16 + RT]
+                h32[q, i * RC + RI : (i + 1) * RC, :] = text[i]
+            TS[1, q] = jnp.concatenate(text, axis=0).astype(BF16)
+        send_text(1)
 
     def down_rest():
         w_step3(3)
@@ -500,11 +545,9 @@
 
     lax.fori_loop(0, NZ + 3, hidden_step, 0)
 
-    img_lane = lax.broadcasted_iota(jnp.int32, (CH, SEQ), 1) < IMG
-    txt_lane = lax.broadcasted_iota(jnp.int32, (CH, 128), 1) >= 64
-    turned = u32[...].T
-    uT[...] = jnp.where(img_lane, turned, 0.0).astype(BF16)
-    uTt[...] = jnp.where(txt_lane, turned[:, SEQ - 128 :], 0.0).astype(BF16)
+    lane = lax.broadcasted_iota(jnp.int32, (CH, SEQ), 1)
+    img_lane = lane % RC < RI
+    uT[...] = jnp.where(img_lane, u32[...].T, 0.0).astype(BF16)
     hc[...] = h32[...].astype(BF16)
 
     total = ndiff[...] + zst[0].astype(F32)
@@ -525,201 +568,235 @@
     send_e(0, 1, zdev(1)).start()
     send_e(0, 2, zdev(-1)).start()
 
-    def err_chunk(i, _):
-        @pl.when(i > 0)
-        def _():
-            send_e(i, i, zdev(1)).wait_recv()
-
-        @pl.when(jnp.logical_and(i > 0, i < 6))
-        def _():
-            send_e(i, i + 2, zdev((i % 2) * 2 - 1)).start()
-
-        full = errz[i].astype(F32)
-        e32[pl.ds(pl.multiple_of(i * RI, 8), RI), :] = full[0:RI]
-        e32[pl.ds(pl.multiple_of(IMG + i * RT, 8), RT), :] = full[RI : RI + RT]
-        return 0
-
-    lax.fori_loop(0, NZ, err_chunk, 0)
-    ec[...] = e32[...].astype(BF16)
-
-    def hg_block(q, _):
-        lanes = pl.ds(pl.multiple_of(q * HQ, HQ), HQ)
-        gi = dot(ec[0:IMG], W[2, :, lanes]).astype(BF16)
-        gt = dot(ec[IMG:SEQ], W[3, :, lanes]).astype(BF16)
-        for j in range(NJ):
-            hgs[j, q, 0:IMG, :] = gi[:, j * HJ : (j + 1) * HJ]
-            hgs[j, q, IMG:SEQ, :] = gt[:, j * HJ : (j + 1) * HJ]
-        return 0
-
-    lax.fori_loop(0, NX, hg_block, 0)
-
-    def rs_hg(j, h):
-        rows = pl.ds(h * 256, 256)
+    def rs_hg(i):
         return Sum(
-            lambda q: hgs.at[j, q, rows], hgr.at[j, 2, rows], lambda k: hgr.at[j, k, rows],
-            lambda k: s_hgs.at[j, h, k], lambda k: s_hgr.at[j, h, k], x, xdev, 1 - 2 * h,
+            lambda q: hgs.at[i, q], hgr.at[i, 2], lambda k: hgr.at[i, k],
+            lambda k: s_hgs.at[i, k], lambda k: s_hgr.at[i, k], x, xdev, sign(i),
         )
 
-    def ag_pg(j, h):
-        rows = pl.ds(h * 256, 256)
-        return Gather(
-            lambda q: pg.at[j, q, rows], lambda k: s_pgs.at[j, h, k], lambda k: s_pgr.at[j, h, k], x, xdev, 1 - 2 * h
-        )
-
-    units = [(j, h) for j in range(NJ) for h in range(2)]
-    for j, h in units:
-        rs_hg(j, h).relayed.start()
-    for j, h in units:
-        rs_hg(j, h).direct.start()
-
-    turned = e32[...].T
-    eT[...] = jnp.where(img_lane, turned, 0.0).astype(BF16)
-    eTt[...] = jnp.where(txt_lane, turned[:, SEQ - 128 :], 0.0).astype(BF16)
-
-    def gd_block(q, _):
-        G[0, q] = dot(eT[...], hc[q]).astype(BF16)
-        G[1, q] = dot(eTt[...], hc[q, SEQ - 128 :, :]).astype(BF16)
-        return 0
-
-    lax.fori_loop(0, NX, gd_block, 0)
-
-    def cols(m, j):
-        return pl.ds(0, HQ) if j is None else pl.ds(j * HJ, HJ)
-
-    def core_cp(p, m, j, l):
-        return remote(
-            G.at[m, l * 2 + 1 - c, :, cols(m, j)], CR.at[m, l, :, cols(m, j)], s_cs.at[p, l], s_cr.at[p, l], core
-        )
-
-    def rs_y(p, m, j, h):
-        rows = pl.ds(h * HR, HR)
-        return Sum(
-            lambda yy: G.at[
-                m, (yy % 2) * 2 + c, pl.ds(pl.multiple_of((yy // 2) * ROWS + h * HR, HR), HR), cols(m, j)
-            ],
-            YR.at[m, 2, rows, cols(m, j)], lambda k: YR.at[m, k, rows, cols(m, j)],
-            lambda k: s_ys.at[p, h, k], lambda k: s_yr.at[p, h, k], y, ydev, 1 - 2 * h,
-        )
-
-    def join_y(p, m, j):
-        for h in range(2):
-            rs_y(p, m, j, h).join()
-
-    def after_core(p, m, j):
-        for l in range(2):
-            core_cp(p, m, j, l).wait_recv()
-            G[m, l * 2 + c, :, cols(m, j)] = (
-                G[m, l * 2 + c, :, cols(m, j)].astype(F32) + CR[m, l, :, cols(m, j)].astype(F32)
-            ).astype(BF16)
-        for h in range(2):
-            rs_y(p, m, j, h).relayed.start()
-        for h in range(2):
-            rs_y(p, m, j, h).direct.start()
-
-    for m in range(2):
-        for l in range(2):
-            core_cp(m, m, None, l).start()
-
-    def pre_grad(j):
-        for h in range(2):
-            rs_hg(j, h).wait()
-        g = hgs[j, x].astype(F32) + hgr[j, 0].astype(F32) + hgr[j, 1].astype(F32)
-        pg[j, x] = (g * gelu_slope(pre_c[:, j * HJ : (j + 1) * HJ])).astype(BF16)
-        for h in range(2):
-            ag_pg(j, h).first()
-
-    def pass_pg(j):
-        for h in range(2):
-            ag_pg(j, h).forward()
-
-    for j, h in units:
-        rs_hg(j, h).join()
-    after_core(0, 0, None)
-    after_core(1, 1, None)
-    pre_grad(0)
-    pre_grad(1)
-    pass_pg(0)
-    join_y(0, 0, None)
-    pre_grad(2)
-    pass_pg(1)
-    join_y(1, 1, None)
-    pass_pg(2)
-
-    for j in range(NJ):
-        for h in range(2):
-            ag_pg(j, h).wait()
-        wide = jnp.concatenate([pg[j, q] for q in range(NX)], axis=1)
-        gi = dot(uT[...], wide).astype(BF16)
-        gt = dot(uTt[...], wide[SEQ - 128 :]).astype(BF16)
-        for q in range(NX):
-            G[2, q, :, j * HJ : (j + 1) * HJ] = gi[:, q * HJ : (q + 1) * HJ]
-            G[3, q, :, j * HJ : (j + 1) * HJ] = gt[:, q * HJ : (q + 1) * HJ]
-        for k in range(2):
-            for l in range(2):
-                core_cp(2 + 2 * j + k, 2 + k, j, l).start()
-        for k in range(2):
-            after_core(2 + 2 * j + k, 2 + k, j)
-        if j > 0:
-            for k in range(2):
-                join_y(2 * j + k, 2 + k, j - 1)
-    for k in range(2):
-        join_y(2 * NJ + k, 2 + k, NJ - 1)
-
-    mine = pl.ds(pl.multiple_of(hi * ROWS, ROWS), ROWS)
-
-    def finish(p, m, j, out):
-        for h in range(2):
-            rs_y(p, m, j, h).wait()
-        g = G[m, lo * 2 + c, mine, cols(m, j)].astype(F32)
-        for k in range(2):
-            g = g + YR[m, k, :, cols(m, j)].astype(F32)
-        out[:, cols(m, j)] = g
-
-    finish(0, 0, None, out_di)
-    finish(1, 1, None, out_dt)
-    for j in range(NJ):
-        finish(2 + 2 * j, 2, j, out_ui)
-        finish(3 + 2 * j, 3, j, out_ut)
-
-    for m in range(4):
-        for p in range(NP):
-            w1(m, p).wait_send()
-            w2(m, p).wait_send()
-            w3(m, p, 0).wait_send()
-            w3(m, p, 1).wait_send()
-
-    def sent(i, _):
+    def ag_pg(i):
+        return Gather(lambda q: pg.at[i, q], lambda k: s_pgs.at[i, k], lambda k: s_pgr.at[i, k], x, xdev, sign(i))
+
+    def pre_grad(i):
+        rs_hg(i).wait()
+        g = hgs[i, x].astype(F32) + hgr[i, 0].astype(F32) + hgr[i, 1].astype(F32)
+        pg[i, x] = (g * gelu_slope(pre_c[pl.ds(pl.multiple_of(i * RC, 8), RC), :])).astype(BF16)
+        ag_pg(i).first()
+
+    def left_forward(i):
         @pl.when(i > 0)
         def _():
             a, b = send_z(i, i, zdev(1))
             a.wait_send()
             b.wait_send()
-            send_e(i, i, zdev(1)).wait_send()
             mz_main(i).wait_send()
             mz_rest(i).wait_send()
 
         rs_img(i).sent()
         ag_img(i).sent()
+
+        @pl.when(i < 4)
+        def _():
+            for p in range(NP):
+                w1_sent(i, p)
+
+    def w1_sent(m, p):
+        rows = wrows(m, 1 - hi, q_mine, p)
+        for ss, rs in (
+            (s_w1s.at[m, p], s_w1r.at[m, p]), (s_w2s.at[m, p], s_w2r.at[m, p]),
+            (s_w3s.at[m, p, 0], s_w3r.at[m, p, 0]), (s_w3s.at[m, p, 1], s_w3r.at[m, p, 1]),
+        ):
+            remote(rows, rows, ss, rs, core).wait_send()
+
+    def err_chunk(i):
+        left_forward(i)
+
+        @pl.when(i > 0)
+        def _():
+            send_e(i, i, zdev(1)).wait_recv()
+
+        @pl.when(jnp.logical_and(i > 0, i < 6))
+        def _():
+            send_e(i, i + 2, zdev((i % 2) * 2 - 1)).start()
+
+        full = errz[i].astype(F32)
+        image = full[0:RI].astype(BF16)
+        text = full[RI:RC].astype(BF16)
+        t32[pl.ds(pl.multiple_of(i * RT, 8), RT), :] = full[RI:RC]
+        for q in range(NX):
+            lanes = slice(q * HQ, (q + 1) * HQ)
+            hgs[i, q] = jnp.concatenate([dot(image, W[2, :, lanes]), dot(text, W[3, :, lanes])], axis=0).astype(BF16)
+        rs_hg(i).first()
+
+    def err_step(k, _):
+        err_chunk(k)
+
+        @pl.when(k >= 2)
+        def _():
+            rs_hg(k - 2).join()
+
+        @pl.when(k >= 4)
+        def _():
+            pre_grad(k - 4)
+
+        @pl.when(k >= 6)
+        def _():
+            ag_pg(k - 6).forward()
+
         return 0
 
-    lax.fori_loop(0, NZ, sent, 0)
+    lax.fori_loop(0, NZ, err_step, 0)
+
+    def cols(j):
+        return pl.ds(j * HJ, HJ)
+
+    def core_cp(m, j, l):
+        return remote(
+            G.at[m, l * 2 + 1 - c, :, cols(j)], CR.at[m, l, :, cols(j)], s_cs.at[m, j, l], s_cr.at[m, j, l], core
+        )
+
+    def rs_y(m, j, h):
+        rows = pl.ds(h * HR, HR)
+        return Sum(
+            lambda yy: G.at[m, (yy % 2) * 2 + c, pl.ds(pl.multiple_of((yy // 2) * ROWS + h * HR, HR), HR), cols(j)],
+            YR.at[m, 2, rows, cols(j)], lambda k: YR.at[m, k, rows, cols(j)],
+            lambda k: s_ys.at[m, j, h, k], lambda k: s_yr.at[m, j, h, k], y, ydev, 1 - 2 * h,
+        )
+
+    def grad(m, j, left, wide):
+        g = dot(left, wide).astype(BF16)
+        for q in range(NX):
+            G[m, q, :, j * HJ : (j + 1) * HJ] = g[:, q * HJ : (q + 1) * HJ]
+        for l in range(2):
+            core_cp(m, j, l).start()
+
+    def after_core(m, j):
+        for l in range(2):
+            core_cp(m, j, l).wait_recv()
+            G[m, l * 2 + c, :, cols(j)] = (
+                G[m, l * 2 + c, :, cols(j)].astype(F32) + CR[m, l, :, cols(j)].astype(F32)
+            ).astype(BF16)
+        for h in range(2):
+            rs_y(m, j, h).relayed.start()
+        for h in range(2):
+            rs_y(m, j, h).direct.start()
+
+    def join_y(m, j):
+        for h in range(2):
+            rs_y(m, j, h).join()
+
+    mine = pl.ds(pl.multiple_of(hi * ROWS, ROWS), ROWS)
+    outs = (out_ui, out_di, out_ut, out_dt)
+
+    def out_cp(o, j):
+        return pltpu.make_async_copy(OB.at[o, :, cols(j)], outs[o].at[:, cols(j)], s_out.at[o, j])
+
+    def finish(m, j):
+        for h in range(2):
+            rs_y(m, j, h).wait()
+        g = G[m, lo * 2 + c, mine, cols(j)].astype(F32)
+        for k in range(2):
+            g = g + YR[m, k, :, cols(j)].astype(F32)
+        OB[1 - m, :, cols(j)] = g
+        out_cp(1 - m, j).start()
+
+    def text_grad(o, fl, fr):
+        left = TA[fl].reshape(8 * TXT, ROWS).astype(F32).T.astype(BF16)
+        OB[o] = dot(left, TA[fr].reshape(8 * TXT, HQ))
+        for j in range(NJ):
+            out_cp(o, j).start()
+
+    eT[...] = jnp.where(img_lane, errz[...].reshape(SEQ, CH).astype(F32).T, 0.0).astype(BF16)
+    for j in range(NJ):
+        grad(0, j, eT[...], jnp.concatenate([hc[q, :, j * HJ : (j + 1) * HJ] for q in range(NX)], axis=1))
+    rs_hg(6).join()
+    rs_hg(7).join()
+    after_core(0, 0)
+    pre_grad(4)
+    after_core(0, 1)
+    pre_grad(5)
+    after_core(0, 2)
+    halves(2)
+    send_text(2)
+    ag_pg(2).forward()
+    ag_pg(3).forward()
+    pre_grad(6)
+    ag_pg(4).forward()
+    pre_grad(7)
+    join_y(0, 0)
+    ag_pg(5).forward()
+    join_y(0, 1)
+    ag_pg(6).forward()
+    join_y(0, 2)
+    ag_pg(7).forward()
+
+    def pg_in(i, _):
+        ag_pg(i).wait()
+        for q in range(NX):
+            h32[q, pl.ds(pl.multiple_of(i * RT, 8), RT), :] = pg[i, q].astype(F32)[RI:RC]
+        return 0
+
+    lax.fori_loop(0, NZ, pg_in, 0)
+    for j in range(NJ):
+        wide = jnp.concatenate([pg[:, q, :, j * HJ : (j + 1) * HJ].reshape(SEQ, HJ) for q in range(NX)], axis=1)
+        grad(1, j, uT[...], wide)
+        if j == 0:
+            TS[3] = h32[:, 0:TXT, :].astype(BF16)
+            send_text(3)
+        if j > 0:
+            after_core(1, j - 1)
+    after_core(1, NJ - 1)
+
+    def left_backward(i, _):
+        @pl.when(i > 0)
+        def _():
+            send_e(i, i, zdev(1)).wait_send()
+
+        rs_hg(i).sent()
+        ag_pg(i).sent()
+        return 0
+
     for h in range(2):
         rs_txt(h).sent()
         ag_txt(h).sent()
-    for j, h in units:
-        rs_hg(j, h).sent()
-        ag_pg(j, h).sent()
-    parts = [(0, 0, None), (1, 1, None)] + [(2 + 2 * j + k, 2 + k, j) for j in range(NJ) for k in range(2)]
-    for p, m, j in parts:
-        for l in range(2):
-            core_cp(p, m, j, l).wait_send()
-        for h in range(2):
-            rs_y(p, m, j, h).sent()
-
-
-def widen(a, b, c, d, oa, ob, oc, od):
-    for src, dst in ((a, oa), (b, ob), (c, oc), (d, od)):
-        dst[...] = src[...]
+    join_y(1, 0)
+    for j in range(NJ):
+        finish(0, j)
+    join_y(1, 1)
+    wait_text(1)
+    wait_text(2)
+    text_grad(3, 2, 1)
+    join_y(1, 2)
+    wait_text(0)
+    wait_text(3)
+    text_grad(2, 0, 3)
+    lax.fori_loop(0, NZ, left_backward, 0)
+    for f in range(4):
+        sent_text(f)
+    for j in range(NJ):
+        finish(1, j)
+
+    for m in range(2):
+        for j in range(NJ):
+            for l in range(2):
+                core_cp(m, j, l).wait_send()
+            for h in range(2):
+                rs_y(m, j, h).sent()
+    for o in range(4):
+        for j in range(NJ):
+            out_cp(o, j).wait()
+
+
+def hand_on(a, b, c, d, oa, ob, oc, od, buf, s_in, s_out):
+    ins = [pltpu.make_async_copy(src, buf.at[i], s_in.at[i]) for i, src in enumerate((a, b, c, d))]
+    outs = [pltpu.make_async_copy(buf.at[i], dst, s_out.at[i]) for i, dst in enumerate((oa, ob, oc, od))]
+    for cp in ins:
+        cp.start()
+    for i in range(4):
+        ins[i].wait()
+        outs[i].start()
+    for cp in outs:
+        cp.wait()
 
 
 def body(
@@ -737,13 +814,12 @@
     smem = pl.BlockSpec(memory_space=pltpu.SMEM)
     V = pltpu.VMEM
     dma = lambda *s: pltpu.SemaphoreType.DMA(s)
-    parts = 2 + 2 * NJ
     out = jax.ShapeDtypeStruct((ROWS, HQ), F32)
     grads = pl.pallas_call(
         kernel,
         out_shape=(out, out, out, out),
         in_specs=[any_] * 8 + [vmem, vmem, smem, smem, smem],
-        out_specs=(vmem,) * 4,
+        out_specs=(any_,) * 4,
         scratch_shapes=[
             V((RI, D), BF16), V((RT, D), BF16), V((RI, D), BF16), V((RT, D), BF16),
             V((4, CH, HB), BF16), V((NZ, 2 * RI, CH), BF16), V((NZ * 16, CH), BF16),
@@ -753,14 +829,15 @@
             V((NZ, NX, 2 * RI, HQ), BF16), V((NX, 128, HQ), BF16),
             V((SEQ, HQ), F32), V((NX, SEQ, HQ), F32), V((NX, SEQ, HQ), BF16),
             V((NZ, 64, CH), BF16), V((NZ, 16, CH), F32), V((NZ, 64, CH), BF16), V((NZ, 64, CH), BF16),
-            V((SEQ, CH), F32), V((SEQ, CH), BF16),
-            V((CH, SEQ), BF16), V((CH, SEQ), BF16), V((CH, 128), BF16), V((CH, 128), BF16),
-            V((NJ, NX, SEQ, HJ), BF16), V((NJ, 3, SEQ, HJ), BF16), V((NJ, NX, SEQ, HJ), BF16),
-            V((4, NX, CH, HQ), BF16), V((4, 2, CH, HQ), BF16), V((4, 3, ROWS, HQ), BF16),
+            V((TXT, CH), F32), V((CH, SEQ), BF16), V((CH, SEQ), BF16),
+            V((NZ, NX, RC, HQ), BF16), V((NZ, 3, RC, HQ), BF16), V((NZ, NX, RC, HQ), BF16),
+            V((2, NX, CH, HQ), BF16), V((2, 2, CH, HQ), BF16), V((2, 3, ROWS, HQ), BF16),
+            V((4, 4, TXT, HQ), BF16), V((4, 2, 4, TXT, HQ), BF16), V((4, ROWS, HQ), F32),
             dma(4), dma(4), dma(4, NP), dma(4, NP), dma(4, NP), dma(4, NP), dma(4, NP, 2), dma(4, NP, 2),
             dma(NZ), dma(NZ), dma(NZ), dma(NZ),
             dma(10, 3), dma(10, 3), dma(10, 3), dma(10, 3), dma(NZ), dma(NZ), dma(NZ), dma(NZ), dma(NZ), dma(NZ),
-            dma(NJ, 2, 3), dma(NJ, 2, 3), dma(NJ, 2, 3), dma(NJ, 2, 3), dma(parts, 2), dma(parts, 2), dma(parts, 2, 3), dma(parts, 2, 3),
+            dma(NZ, 3), dma(NZ, 3), dma(NZ, 3), dma(NZ, 3), dma(2, NJ, 2), dma(2, NJ, 2),
+            dma(2, NJ, 2, 3), dma(2, NJ, 2, 3), dma(4, 4, 2), dma(4, 4, 2), dma(4, NJ),
         ],
         compiler_params=pltpu.CompilerParams(
             collective_id=0, has_side_effects=True, vmem_limit_bytes=60 * 1024 * 1024
@@ -770,7 +847,8 @@
         modulation, feats, timesteps, skips, text_lengths,
     )
     return pl.pallas_call(
-        widen, out_shape=(out, out, out, out), in_specs=[vmem] * 4, out_specs=(vmem,) * 4,
+        hand_on, out_shape=(out, out, out, out), in_specs=[any_] * 4, out_specs=(any_,) * 4,
+        scratch_shapes=[V((4, ROWS, HQ), F32), dma(4), dma(4)],
     )(*grads)
 
 

time: 166 us -> 149 us (0.90)
  Pallas kernels: 163 us -> 145 us
    pallas_call x1, Pallas kernels: 160 us -> 142 us  [body(): pl.pallas_call(kernel, out_shape=(out, out, out, out), in_specs=[any_] *...]
where the time goes in v3:
time: 149 us; the launch traced here: 148 us
  Pallas kernels  145 us (97%)
  other arithmetic  1.68 us (1%)
    pallas_call x1, Pallas kernels, body(): pl.pallas_call(kernel, out_shape=(out, out, out, out), in_specs=[any_] *...  142 us

profile of v3, /device:TPU:1, one launch (start us, length us, event | category | flops | bytes accessed | tf_op | source)
XLA Modules:
  0.0 148.0 jit_solution(5333432915053911570)
XLA Ops:
  0.6 0.7 sub.3
  1.3 0.7 add_convert_fusion
  2.0 0.3 multiply_cosine_fusion
  2.3 0.7 broadcast_in_dim.2.feats
  3.0 142.5 %shard_map.147 = (f32[384,384]{1,0:T(8,128)}, f32[384,384]{1,0:T(8,128)}, f32[384,384]{1,0:T(8,128)}, f32[384,384]{1,0:T(8,128)}) custom-call(bf16[2,56,3072]{2,1,0:T(8,128)(2,1)} %lat_i.1, bf16[2,8,3072]{2,1,0:T(8,128)(2,1)} %lat_t.1, bf16[2,56,3072]{2,1,0:T(8,128)(2,1)} %noi_i.1, bf16[2,8,3072]{2,1,0:T(8,128)(2,1)} %noi_t.1, bf16[384,1536]{1,0:T(8,128)(2,1)} %up_i.1, ...), custom_call_target="tpu_custom_call" | custom-call | tf_op jit(solution)/shard_map/pallas_call | solution.py:818
  145.5 2.5 %shard_map.148 = (f32[384,384]{1,0:T(8,128)}, f32[384,384]{1,0:T(8,128)}, f32[384,384]{1,0:T(8,128)}, f32[384,384]{1,0:T(8,128)}) custom-call(f32[384,384]{1,0:T(8,128)} %get-tuple-element.8.a, f32[384,384]{1,0:T(8,128)} %get-tuple-element.9.b, f32[384,384]{1,0:T(8,128)} %get-tuple-element.10.c, f32[384,384]{1,0:T(8,128)} %get-tuple-element.11.d), custom_call_target="tpu_custom_call" | custom-call | tf_op jit(solution)/shard_map/pallas_call | solution.py:849
  (2 shorter events, 0.0 us)

commit v4 on v3

v4 whole, which is shorter than its diff:
```python
import functools
import math

import jax
import jax.numpy as jnp
from jax import lax
from jax.experimental import pallas as pl
from jax.experimental.pallas import tpu as pltpu
from jax.sharding import PartitionSpec as P

D = 3072
FF = 12288
IMG = 448
TXT = 64
STEPS = 1000
SEQ = 512
SAMPLES = 8

NX = 4
NZ = 8
CH = D // NX
HB = FF // NZ
HQ = HB // NX
RI = IMG // NZ
RT = TXT // NZ
RC = RI + RT
NJ = 3
LAG = 2
HJ = HQ // NJ
ROWS = D // 8
QR = ROWS // 4
HR = ROWS // 2

GELU_SCALE = 0.7978845608028654
GELU_CUBIC = 0.044715
NORM_EPS = 1e-06
MESH = pl.DeviceIdType.MESH
F32 = jnp.float32
BF16 = jnp.bfloat16


def gelu_tanh(values):
    inner = GELU_SCALE * (values + GELU_CUBIC * values * values * values)
    return 0.5 * values * (1.0 + jnp.tanh(inner))


def gelu_slope(values):
    inner = GELU_SCALE * (values + GELU_CUBIC * values * values * values)
    tangent = jnp.tanh(inner)
    return 0.5 * (1.0 + tangent) + 0.5 * values * (1.0 - tangent * tangent) * GELU_SCALE * (
        1.0 + 3.0 * GELU_CUBIC * values * values
    )


def dot(a, b):
    return jnp.dot(a, b, preferred_element_type=F32)


def dot_nt(a, b):
    return lax.dot_general(a, b, (((1,), (1,)), ((), ())), preferred_element_type=F32)


class Sum:
    def __init__(self, part, relay, got, both, ss, rs, pos, to, s):
        self.part, self.relay, self.got, self.both = part, relay, got, both
        self.ss, self.rs, self.pos, self.to, self.s = ss, rs, pos, to, s

    @property
    def relayed(self):
        return remote(self.part((self.pos + 2) % 4), self.relay, self.ss, self.rs[0], self.to(self.s))

    @property
    def direct(self):
        return remote(self.part((self.pos - self.s + 4) % 4), self.got(0), self.ss, self.rs[1], self.to(-self.s))

    @property
    def joined(self):
        return remote(self.part((self.pos + self.s + 4) % 4), self.got(1), self.ss, self.rs[1], self.to(self.s))

    def add(self):
        joint = self.part((self.pos + self.s + 4) % 4)
        joint[...] = (joint[...].astype(F32) + self.relay[...].astype(F32)).astype(BF16)
        self.joined.start()

    def join(self):
        self.relayed.wait_recv()
        self.add()

    def first(self):
        self.relayed.start()
        self.direct.start()

    def wait(self):
        remote(self.both, self.both, self.ss, self.rs[1], self.to(1)).wait_recv()


class Gather:
    def __init__(self, slot, both, ss, rs, pos, to, s):
        self.slot, self.both, self.ss, self.rs, self.pos, self.to, self.s = slot, both, ss, rs, pos, to, s

    @property
    def plus(self):
        return remote(self.slot(self.pos), self.slot(self.pos), self.ss, self.rs[0], self.to(self.s))

    @property
    def minus(self):
        return remote(self.slot(self.pos), self.slot(self.pos), self.ss, self.rs[1], self.to(-self.s))

    @property
    def onward(self):
        back = self.slot((self.pos - self.s + 4) % 4)
        return remote(back, back, self.ss, self.rs[1], self.to(self.s))

    def first(self):
        self.plus.start()
        self.minus.start()

    def forward(self):
        self.plus.wait_recv()
        self.onward.start()

    def wait(self):
        remote(self.both, self.both, self.ss, self.rs[1], self.to(1)).wait_recv()


def remote(src, dst, ss, rs, who):
    return pltpu.make_async_remote_copy(
        src_ref=src, dst_ref=dst, send_sem=ss, recv_sem=rs, device_id=who, device_id_type=MESH
    )


def kernel(
    lat_i, lat_t, noi_i, noi_t, up_i, up_t, dn_i, dn_t, modulation, timesteps, skips, lengths,
    out_ui, out_di, out_ut, out_dt,
    lbi, lbt, nbi, nbt, W, uall, ndiff, mod, coef, u32,
    stg, stgt, rrs, rrst, hid, hidt, pre_c, h32, hc,
    zst, rem, zr, errz, t32, uT, eT, hgs, hgr, pg, G, CR, YR, TS, TA, OB,
    s_loc, s_wl, s_w1, s_w2, s_w3, s_z, s_rs, s_rst, s_ag, s_agt, s_mz, s_ez, s_hg, s_pge, s_pgeg, s_pg, s_pgg, s_core, s_y, s_t, s_out, s_sent,
):
    r = lax.axis_index("row")
    z = lax.axis_index("col")
    d = lax.axis_index("dp")
    x, hi, lo, c = r // 2, r % 2, d // 2, d % 2
    y = hi * 2 + lo

    def dev(x, hi, lo, c, z):
        return (x * 2 + hi, z, lo * 2 + c)

    def xdev(t):
        return dev((x + t + NX) % NX, hi, lo, c, z)

    def zdev(t):
        return dev(x, hi, lo, c, (z + t + NZ) % NZ)

    def ydev(t):
        yy = (y + t + 4) % 4
        return dev(x, yy // 2, yy % 2, c, z)

    def tdev(t, k):
        yy = (y + t) % 4
        return dev(x, yy // 2, yy % 2, c + k - 2 * c * k, z)

    core = dev(x, hi, lo, 1 - c, z)
    adj = dev(x, 1 - hi, 1 - lo, c, z)
    side = dev(x, hi, 1 - lo, c, z)

    bar = pltpu.get_barrier_semaphore()
    for t in range(1, NX):
        pl.semaphore_signal(bar, inc=1, device_id=xdev(t), device_id_type=MESH)
    for t in range(1, NZ):
        pl.semaphore_signal(bar, inc=1, device_id=zdev(t), device_id_type=MESH)
    others = [(t, k) for t in range(4) for k in range(2) if t or k]
    for t, k in others:
        pl.semaphore_signal(bar, inc=1, device_id=tdev(t, k), device_id_type=MESH)

    reads = [
        pltpu.make_async_copy(lat_i.at[hi], lbi, s_loc.at[0]),
        pltpu.make_async_copy(lat_t.at[hi], lbt, s_loc.at[1]),
        pltpu.make_async_copy(noi_i.at[hi], nbi, s_loc.at[2]),
        pltpu.make_async_copy(noi_t.at[hi], nbt, s_loc.at[3]),
    ]
    for cp in reads:
        cp.start()
    weights = (up_i, up_t, dn_i, dn_t)
    wl = [
        pltpu.make_async_copy(
            weights[m], W.at[m, pl.ds(pl.multiple_of(hi * ROWS, ROWS), ROWS)], s_wl.at[m]
        )
        for m in range(4)
    ]

    q_mine = lo * 2 + c
    q_side = (1 - lo) * 2 + c

    def wpiece(m, half, quarter, p):
        rows = pl.ds(pl.multiple_of(half * ROWS + quarter * QR, QR), QR)
        return W.at[m, rows, first_lanes(p)] if m == 0 else W.at[m, rows]

    def first_q(p):
        return (x + (2, 1, 3, 0)[p]) % NX

    def first_lanes(p):
        return pl.ds(pl.multiple_of(first_q(p) * HQ, HQ), HQ)

    def widx(m, p):
        return p if m == 0 else 3 + m

    def w1(m, p):
        rows = pl.ds(pl.multiple_of(q_side * QR, QR), QR)
        src = weights[m].at[rows, first_lanes(p)] if m == 0 else weights[m].at[rows]
        return remote(src, wpiece(m, hi, q_side, p), s_sent.at[0], s_w1.at[widx(m, p)], adj)

    def w2(m, p):
        piece = wpiece(m, 1 - hi, q_mine, p)
        return remote(piece, piece, s_sent.at[1], s_w2.at[widx(m, p)], side)

    def w3(m, p, k):
        piece = wpiece(m, 1 - hi, q_side if k else q_mine, p)
        return remote(piece, piece, s_sent.at[2], s_w3.at[widx(m, p)], core)

    def w_step1(m, p=0):
        w1(m, p).wait_recv()
        w2(m, p).start()
        w3(m, p, 0).start()

    def w_step2(m, p=0):
        w2(m, p).wait_recv()
        w3(m, p, 1).start()

    def w_step3(m, p=0):
        if p == 0:
            wl[m].wait()
        both = W.at[m, 0 : 2 * QR, 0:HQ] if m == 0 else W.at[m, 0 : 2 * QR]
        remote(both, both, s_sent.at[2], s_w3.at[widx(m, p)], core).wait_recv()

    for cp in wl:
        cp.start()
    lane0 = pl.multiple_of(x * CH, CH)
    own_lanes = pl.ds(lane0, CH)
    t_s = timesteps[hi]
    t_g = t_s - skips[hi]
    times = (t_s.astype(F32), t_g.astype(F32))
    lane = lax.broadcasted_iota(jnp.int32, (8, CH), 1) + (x * CH) % (D // 2)
    frequency = jnp.exp(-math.log(10000.0) * lane.astype(F32) / (D // 2))
    angles = frequency * jnp.where(lax.broadcasted_iota(jnp.int32, (8, CH), 0) == 0, times[0], times[1])
    feats = jnp.where(lane * 0 + x < NX // 2, jnp.cos(angles), jnp.sin(angles))
    for k in range(2):
        for a in range(3):
            for b in range(2):
                mod[k, a, b : b + 1, :] = (
                    modulation[k, a, 0:1, own_lanes] + modulation[k, a, 1:2, own_lanes] * feats[b : b + 1]
                )
    levels = (times[0] * (1.0 / STEPS), times[1] * (1.0 / STEPS))
    length = lengths[hi]
    row = lax.broadcasted_iota(jnp.int32, (RI + RT, 128), 0)
    valid = jnp.logical_or(row < RI, row + (z * RT - RI) < length)
    count = jnp.full((RI + RT, 128), IMG, F32) + length.astype(F32)
    coef[...] = jnp.where(valid, SEQ / math.sqrt(SAMPLES * SEQ) / count, 0.0)
    pl.semaphore_wait(bar, 17)
    for p in range(NX):
        w1(0, p).start()
    for cp in reads:
        cp.wait()
    for latb, noib, rows, stream, base in ((lbi, nbi, RI, 0, 0), (lbt, nbt, RT, 1, RI)):
        lat_own = latb[:, own_lanes].astype(F32)
        noi_own = noib[:, own_lanes].astype(F32)
        owns = []
        us = []
        for b in range(2):
            level = levels[b]
            full = (1.0 - level) * latb[...].astype(F32) + level * noib[...].astype(F32)
            mean = jnp.mean(full, axis=-1, keepdims=True)
            cen = full - mean
            var = jnp.mean(cen * cen, axis=-1, keepdims=True)
            own = (1.0 - level) * lat_own + level * noi_own
            owns.append(own)
            normed = (own - mean) * lax.rsqrt(var + NORM_EPS)
            us.append(normed * (1.0 + mod[stream, 1, b : b + 1, :]) + mod[stream, 0, b : b + 1, :])
        ndiff[base : base + rows, :] = owns[0] - owns[1]
        both = jnp.concatenate(us, axis=0).astype(BF16)
        uall[0, 2 * base : 2 * (base + rows), :] = both

    def send_z(i, to, p, who):
        rows = pl.ds(p * RC, RC)
        return remote(uall.at[i, rows], uall.at[to, rows], s_sent.at[3], s_z.at[to, p], who)

    for p in range(2):
        send_z(0, 1, p, zdev(1)).start()
        send_z(0, 2, p, zdev(-1)).start()

    def z_pass(*chunks):
        for p in range(2):
            for i in chunks:
                send_z(i, i, p, zdev(1)).wait_recv()
                if i < 6:
                    send_z(i, i + 2, p, zdev((i % 2) * 2 - 1)).start()

    def sign(i):
        return 1 - 2 * (i % 2)

    def rs_img(i):
        return Sum(
            lambda q: stg.at[i, q], rrs.at[i, 2], lambda k: rrs.at[i, k], rrs.at[i, 0:2],
            s_sent.at[4], (s_rs.at[i, 0], s_rs.at[i, 1]), x, xdev, sign(i),
        )

    def ag_img(i):
        return Gather(
            lambda q: hid.at[i, q], rrs.at[i, 0:2], s_sent.at[5], (s_ag.at[i, 0], s_ag.at[i, 1]), x, xdev, sign(i)
        )

    def rs_txt(h):
        rows = pl.ds(h * 64, 64)
        return Sum(
            lambda q: stgt.at[q, rows], rrst.at[2, rows], lambda k: rrst.at[k, rows], rrst.at[0:2, rows],
            s_sent.at[6], (s_rst.at[h, 0], s_rst.at[h, 1]), x, xdev, 1 - 2 * h,
        )

    def ag_txt(h):
        rows = pl.ds(h * 64, 64)
        return Gather(
            lambda q: hidt.at[q, rows], rrst.at[0:2, rows], s_sent.at[7], (s_agt.at[h, 0], s_agt.at[h, 1]),
            x, xdev, 1 - 2 * h,
        )

    def up_first(p):
        w_step3(0, p)
        for i in range(3):
            stg[i, first_q(p)] = dot(uall[i, 0 : 2 * RI], W[0, :, first_lanes(p)]).astype(BF16)
        if p == 0:
            for i in range(3):
                rs_img(i).relayed.start()
        elif p == 1:
            rs_img(1).direct.start()
        elif p == 2:
            rs_img(0).direct.start()
            rs_img(2).direct.start()

    w_step1(0, 0)
    w_step1(0, 1)
    z_pass(1, 2)
    w_step2(0, 0)
    w_step1(0, 2)
    w_step2(0, 1)
    up_first(0)
    w_step1(0, 3)
    for m in range(1, 4):
        w1(m, 0).start()
    z_pass(3, 4)
    w_step2(0, 2)
    up_first(1)
    w_step2(0, 3)
    up_first(2)
    up_first(3)
    for i in range(3):
        rs_img(i).join()

    def up_chunk(i):
        u = uall[i, 0 : 2 * RI]
        for q in range(NX):
            stg[i, q] = dot(u, W[0, :, q * HQ : (q + 1) * HQ]).astype(BF16)
        rs_img(i).first()

    def at(k, step, do, *args):
        @pl.when(k == step)
        def _():
            do(*args)

    def up_step(k, _):
        at(k, 4, z_pass, 5, 6)
        at(k, 6, z_pass, 7)

        @pl.when(k < NZ)
        def _():
            up_chunk(k)

        at(k, 4, w_step1, 1)
        at(k, 5, w_step1, 2)
        at(k, 6, w_step2, 1)
        at(k, 7, w_step1, 3)

        @pl.when(k > 3)
        def _():
            rs_img(k - 1).join()

        return 0

    lax.fori_loop(3, NZ + 1, up_step, 0)
    w_step2(2)

    w_step3(1)
    utxt = uall[:, 2 * RI :].reshape(NZ * 16, CH)
    for q in range(NX):
        stgt[q] = dot(utxt, W[1, :, q * HQ : (q + 1) * HQ]).astype(BF16)
    for h in range(2):
        rs_txt(h).first()

    def pack_u(i, _):
        u32[pl.ds(pl.multiple_of(i * RC, 8), RI), :] = uall[i, 0 : 2 * RI].astype(F32)[0:RI]
        text = uall[i, 2 * RI :].astype(F32)[0:RT]
        u32[pl.ds(pl.multiple_of(i * RC + RI, 8), RT), :] = text
        t32[pl.ds(pl.multiple_of(i * RT, 8), RT), :] = text
        return 0

    lax.fori_loop(0, NZ, pack_u, 0)

    def text_cp(f, t, k, rows, lanes):
        yy = (y + t) % 4
        b = yy // 2 if f % 2 == 0 else (yy % 2) * 2 + c + k - 2 * c * k
        return remote(TS.at[f, b, rows, lanes], TA.at[f, k, t, rows, lanes], s_sent.at[8], s_t.at[f], tdev(t, k))

    def send_text(f, rows=slice(0, TXT), lanes=slice(0, HQ)):
        TA[f, 0, 0, rows, lanes] = TS[f, hi if f % 2 == 0 else q_mine, rows, lanes]
        for t, k in others:
            text_cp(f, t, k, rows, lanes).start()

    def wait_text(f):
        seven = TA.at[f].reshape(8, TXT, HQ).at[0:7]
        remote(seven, seven, s_sent.at[8], s_t.at[f], core).wait_recv()

    def halves(f, rows=slice(0, TXT)):
        for h in range(2):
            TS[f, h, rows] = t32[rows, h * ROWS : (h + 1) * ROWS].astype(BF16)

    halves(0)

    def act_chunk(i):
        rs_img(i).wait()
        pre = stg[i, x].astype(F32) + rrs[i, 0].astype(F32) + rrs[i, 1].astype(F32)
        pre_c[pl.ds(pl.multiple_of(i * RC, 8), RI), :] = pre[0:RI]
        hid[i, x] = gelu_tanh(pre).astype(BF16)
        ag_img(i).first()

    def join_text():
        for h in range(2):
            rs_txt(h).join()

    def act_text():
        for h in range(2):
            rs_txt(h).wait()
        pre = stgt[x].astype(F32) + rrst[0].astype(F32) + rrst[1].astype(F32)
        for i in range(NZ):
            pre_c[i * RC + RI : (i + 1) * RC, :] = pre[i * 16 : i * 16 + RT]
        hidt[x] = gelu_tanh(pre).astype(BF16)
        for h in range(2):
            ag_txt(h).first()

    def pass_text():
        for h in range(2):
            ag_txt(h).forward()

    def zslot(i):
        half = (i + 1) // 2
        return (NZ + half - 2 * half * (i % 2)) % NZ

    def mz(i, rows):
        return remote(zst.at[i, rows], zr.at[zslot(i), rows], s_sent.at[9], s_mz, zdev(zslot(i)))

    def mz_main(i):
        return mz(i, pl.ds(0, 48))

    def mz_rest(i):
        return mz(i, pl.ds(48, 16))

    def down_chunk(i):
        ag_img(i).wait()
        out = dot_nt(hid[i, 0], W[2, :, 0:HQ])
        for q in range(1, NX):
            out = out + dot_nt(hid[i, q], W[2, :, q * HQ : (q + 1) * HQ])
        diff = mod[0, 2, 0:1, :] * out[0:RI] - mod[0, 2, 1:2, :] * out[RI : 2 * RI]
        zst[i, 0:48, :] = diff[0:48].astype(BF16)
        rem[i, 0:8, :] = diff[48:56]

        @pl.when(i > 0)
        def _():
            mz_main(i).start()

        for q in range(NX):
            h32[q, pl.ds(pl.multiple_of(i * RC, 8), RI), :] = hid[i, q].astype(F32)[0:RI]

    def rest_chunk(i, _):
        zst[i, 48:64, :] = rem[i].astype(BF16)

        @pl.when(i > 0)
        def _():
            mz_rest(i).start()

        return 0

    def down_text():
        for h in range(2):
            ag_txt(h).wait()
        out = dot_nt(hidt[0], W[3, :, 0:HQ])
        for q in range(1, NX):
            out = out + dot_nt(hidt[q], W[3, :, q * HQ : (q + 1) * HQ])
        for i in range(NZ):
            rem[i, 8:16, :] = (
                mod[1, 2, 0:1, :] * out[i * 16 : i * 16 + RT] - mod[1, 2, 1:2, :] * out[i * 16 + RT : (i + 1) * 16]
            )
        for q in range(NX):
            full = hidt[q].astype(F32)
            text = [full[i * 16 : i * 16 + RT] for i in range(NZ)]
            for i in range(NZ):
                h32[q, i * RC + RI : (i + 1) * RC, :] = text[i]
            TS[1, q] = jnp.concatenate(text, axis=0).astype(BF16)
        send_text(1)

    def down_rest():
        w_step3(3)
        down_text()
        lax.fori_loop(5, NZ, rest_chunk, 0)

    def order(k):
        return k + 5 * (1 - (k + 5) // 8) + (k // 5) * (7 - 2 * k)

    def hidden_step(k, _):
        @pl.when(k < NZ)
        def _():
            act_chunk(order(k))

        at(k, 1, join_text)
        at(k, 3, act_text)

        @pl.when(jnp.logical_and(k >= LAG, k < NZ + LAG))
        def _():
            ag_img(order(k - LAG)).forward()

        at(k, LAG + 1, w_step2, 3)
        at(k, LAG + 1, w_step3, 2)
        at(k, LAG + 3, pass_text)

        @pl.when(k >= LAG + 2)
        def _():
            down_chunk(order(k - LAG - 2))

        at(k, LAG + 4, down_rest)
        at(k, LAG + 5, send_text, 0)

        @pl.when(k >= LAG + 5)
        def _():
            rest_chunk(order(k - LAG - 2), 0)

        return 0

    lax.fori_loop(0, NZ + LAG + 2, hidden_step, 0)

    lane = lax.broadcasted_iota(jnp.int32, (CH, SEQ), 1)
    img_lane = lane % RC < RI
    uT[...] = jnp.where(img_lane, u32[...].T, 0.0).astype(BF16)
    hc[...] = h32[...].astype(BF16)
    pre_c[...] = gelu_slope(pre_c[...])

    total = ndiff[...] + zst[0].astype(F32)
    remote(zr.at[1:NZ], zr.at[1:NZ], s_sent.at[9], s_mz, core).wait_recv()
    for s in range(1, NZ):
        total = total + zr[s].astype(F32)
    total = total * coef[:, 0:1]
    err_i = mod[0, 2, 0:1, :] * total[0:RI]
    err_t = mod[1, 2, 0:1, :] * total[RI : RI + RT]
    errz[0] = jnp.concatenate([err_i, err_t], axis=0).astype(BF16)

    def send_e(i, to, p, who):
        rows = pl.ds(p * 32, 32)
        return remote(errz.at[i, rows], errz.at[to, rows], s_sent.at[10], s_ez.at[to, p], who)

    for p in range(2):
        send_e(0, 1, p, zdev(1)).start()
        send_e(0, 2, p, zdev(-1)).start()

    def rs_hg(i):
        return Sum(
            lambda q: hgs.at[i, q], hgr.at[2, i], lambda k: hgr.at[k, i], hgr.at[0:2, i],
            s_sent.at[11], (s_hg.at[i, 0], s_hg.at[i, 1]), x, xdev, sign(i),
        )

    def ag_early(i):
        rows = pl.ds(pl.multiple_of(i * RC, RC), RC)
        return Gather(
            lambda q: pg.at[:, q, rows], None, s_sent.at[12], (s_pge.at[i], s_pgeg), x, xdev, sign(i)
        )

    def ag_late(j, h):
        rows = pl.ds(SEQ // 2 + h * (SEQ // 4), SEQ // 4)
        return Gather(
            lambda q: pg.at[j, q, rows], pg.at[j, 0:2, rows], s_sent.at[12], (s_pg.at[j, h], s_pgg.at[j, h]),
            x, xdev, 1 - 2 * h,
        )

    def pre_early(i):
        rs_hg(i).wait()
        g = hgs[i, x].astype(F32) + hgr[0, i].astype(F32) + hgr[1, i].astype(F32)
        rows = pl.ds(pl.multiple_of(i * RC, RC), RC)
        g = (g * pre_c[rows, :]).astype(BF16)
        for j in range(NJ):
            pg[j, x, rows, :] = g[:, j * HJ : (j + 1) * HJ]
        ag_early(i).first()

    def pre_late(j):
        lanes = slice(j * HJ, (j + 1) * HJ)
        late = slice(NZ // 2, NZ)
        g = hgs[late, x, :, lanes].astype(F32) + hgr[0, late, :, lanes].astype(F32) + hgr[1, late, :, lanes].astype(F32)
        pg[j, x, SEQ // 2 :, :] = (g.reshape(SEQ // 2, HJ) * pre_c[SEQ // 2 :, lanes]).astype(BF16)
        for h in range(2):
            ag_late(j, h).first()

    def pass_late(j):
        for h in range(2):
            ag_late(j, h).forward()

    def err_pass(i, p):
        send_e(i, i, p, zdev(1)).wait_recv()

        @pl.when(i < 6)
        def _():
            send_e(i, i + 2, p, zdev((i % 2) * 2 - 1)).start()

    def err_chunk(i):
        full = errz[i].astype(F32)
        image = full[0:RI].astype(BF16)
        text = full[RI:RC].astype(BF16)
        t32[pl.ds(pl.multiple_of(i * RT, 8), RT), :] = full[RI:RC]
        for q in range(NX):
            lanes = slice(q * HQ, (q + 1) * HQ)
            hgs[i, q] = jnp.concatenate([dot(image, W[2, :, lanes]), dot(text, W[3, :, lanes])], axis=0).astype(BF16)
        rs_hg(i).first()

    err_chunk(0)

    def err_step(k, _):
        for p in range(2):
            err_pass(2 * k - 1, p)

            @pl.when(k < 4)
            def _():
                err_pass(2 * k, p)

        err_chunk(2 * k - 1)

        @pl.when(k < 4)
        def _():
            err_chunk(2 * k)

        for i in (3, 2):

            @pl.when(2 * k - i >= 0)
            def _():
                rs_hg(2 * k - i).join()

        at(k, 2, pre_early, 0)
        at(k, 3, pre_early, 1)
        at(k, 3, pre_early, 2)
        at(k, 4, pre_early, 3)

        @pl.when(k >= 3)
        def _():
            ag_early(k - 3).forward()

        @pl.when(k == 3)
        def _():
            halves(2, slice(0, 32))
            send_text(2, slice(0, 32))

        return 0

    lax.fori_loop(1, 5, err_step, 0)
    halves(2, slice(32, TXT))
    send_text(2, slice(32, TXT))

    def cols(j):
        return pl.ds(j * HJ, HJ)

    def core_cp(m, j, l):
        return remote(G.at[m, l * 2 + 1 - c, :, cols(j)], CR.at[m, l, :, cols(j)], s_sent.at[13], s_core.at[m, j], core)

    def rs_y(m, j, h):
        rows = pl.ds(h * HR, HR)
        return Sum(
            lambda yy: G.at[m, (yy % 2) * 2 + c, pl.ds(pl.multiple_of((yy // 2) * ROWS + h * HR, HR), HR), cols(j)],
            YR.at[m, 2, rows, cols(j)], lambda k: YR.at[m, k, rows, cols(j)], None,
            s_sent.at[14], (s_y.at[m, j, 0], s_y.at[m, j, 1]), y, ydev, 1 - 2 * h,
        )

    def grad(m, j, left, wide):
        g = dot(left, wide).astype(BF16)
        for q in range(NX):
            G[m, q, :, j * HJ : (j + 1) * HJ] = g[:, q * HJ : (q + 1) * HJ]
        for l in range(2):
            core_cp(m, j, l).start()

    def after_core(m, j):
        both = CR.at[m, :, :, cols(j)]
        remote(both, both, s_sent.at[13], s_core.at[m, j], core).wait_recv()
        for l in range(2):
            G[m, l * 2 + c, :, cols(j)] = (
                G[m, l * 2 + c, :, cols(j)].astype(F32) + CR[m, l, :, cols(j)].astype(F32)
            ).astype(BF16)
        for h in range(2):
            rs_y(m, j, h).relayed.start()
        for h in range(2):
            rs_y(m, j, h).direct.start()

    def join_y(m, j):
        both = YR.at[m, 2, :, cols(j)]
        remote(both, both, s_sent.at[14], s_y.at[m, j, 0], core).wait_recv()
        for h in range(2):
            rs_y(m, j, h).add()

    mine = pl.ds(pl.multiple_of(hi * ROWS, ROWS), ROWS)
    outs = (out_ui, out_di, out_ut, out_dt)

    def out_cp(o, j):
        return pltpu.make_async_copy(OB.at[o, :, cols(j)], outs[o].at[:, cols(j)], s_out.at[o])

    def finish(m, j):
        both = YR.at[m, 0:2, :, cols(j)]
        remote(both, both, s_sent.at[14], s_y.at[m, j, 1], core).wait_recv()
        g = G[m, lo * 2 + c, mine, cols(j)].astype(F32)
        for k in range(2):
            g = g + YR[m, k, :, cols(j)].astype(F32)
        OB[1 - m, :, cols(j)] = g
        out_cp(1 - m, j).start()

    def text_grad(o, fl, fr):
        left = TA[fl].reshape(8 * TXT, ROWS).astype(F32).T.astype(BF16)
        OB[o] = dot(left, TA[fr].reshape(8 * TXT, HQ))
        for j in range(NJ):
            out_cp(o, j).start()

    eT[...] = jnp.where(img_lane, errz[...].reshape(SEQ, CH).astype(F32).T, 0.0).astype(BF16)
    for j in range(NJ):
        grad(0, j, eT[...], jnp.concatenate([hc[q, :, j * HJ : (j + 1) * HJ] for q in range(NX)], axis=1))
    rs_hg(7).join()
    ag_early(2).forward()
    for j in range(NJ):
        after_core(0, j)
    ag_early(3).forward()
    for i in range(NZ // 2, NZ):
        rs_hg(i).wait()
    for j in range(NJ):
        pre_late(j)
    early = pg.at[:, 0:2, 0 : SEQ // 2]
    remote(early, early, s_sent.at[12], s_pgeg, core).wait_recv()
    for j in range(NJ):
        pass_late(j)
        join_y(0, j)

    def pg_in(j):
        for h in range(2):
            ag_late(j, h).wait()
        lanes = slice(j * HJ, (j + 1) * HJ)
        for q in range(NX):
            text = pg[j, q].astype(F32).reshape(NZ, RC, HJ)[:, RI:RC]
            TS[3, q, :, lanes] = text.reshape(TXT, HJ).astype(BF16)
        return lanes

    for j in range(NJ):
        lanes = pg_in(j)
        grad(1, j, uT[...], jnp.concatenate([pg[j, q] for q in range(NX)], axis=1))
        after_core(1, j)
        send_text(3, lanes=lanes)

    join_y(1, 0)
    for j in range(NJ):
        finish(0, j)
    join_y(1, 1)
    wait_text(1)
    wait_text(2)
    text_grad(3, 2, 1)
    join_y(1, 2)
    wait_text(0)
    wait_text(3)
    text_grad(2, 0, 3)
    for j in range(NJ):
        finish(1, j)

    sent = (
        W.at[:, 0:QR], W.at[:, 0:QR], W.at[:, 0 : 2 * QR], uall.at[0:7], rrs, rrs, rrst, rrst,
        hgs.at[0:7], zst.at[0:7], errz.at[0:7], hgr, hgr, CR, YR,
    )
    for k, whole in enumerate(sent):
        remote(whole, whole, s_sent.at[k], s_sent.at[k], core).wait_send()
    for o in range(4):
        pltpu.make_async_copy(OB.at[o], outs[o], s_out.at[o]).wait()


def hand_on(a, b, c, d, oa, ob, oc, od, buf, s_in, s_out):
    ins = [pltpu.make_async_copy(src, buf.at[i], s_in.at[i]) for i, src in enumerate((a, b, c, d))]
    outs = [pltpu.make_async_copy(buf.at[i], dst, s_out.at[i]) for i, dst in enumerate((oa, ob, oc, od))]
    for cp in ins:
        cp.start()
    for i in range(4):
        ins[i].wait()
        outs[i].start()
    for cp in outs:
        cp.wait()


def body(
    latent_image, latent_text, noise_image, noise_text, up_image, down_image, up_text, down_text,
    modulation, timesteps, skips, text_lengths,
):
    any_ = pl.BlockSpec(memory_space=pl.ANY)
    vmem = pl.BlockSpec(memory_space=pltpu.VMEM)
    smem = pl.BlockSpec(memory_space=pltpu.SMEM)
    V = pltpu.VMEM
    dma = lambda *s: pltpu.SemaphoreType.DMA(s)
    out = jax.ShapeDtypeStruct((ROWS, HQ), F32)
    grads = pl.pallas_call(
        kernel,
        out_shape=(out, out, out, out),
        in_specs=[any_] * 8 + [vmem, smem, smem, smem],
        out_specs=(any_,) * 4,
        scratch_shapes=[
            V((RI, D), BF16), V((RT, D), BF16), V((RI, D), BF16), V((RT, D), BF16),
            V((4, CH, HB), BF16), V((NZ, 2 * RC, CH), BF16),
            V((RI + RT, CH), F32), V((2, 3, 2, CH), F32), V((RI + RT, 128), F32), V((SEQ, CH), F32),
            V((NZ, NX, 2 * RI, HQ), BF16), V((NX, 128, HQ), BF16),
            V((NZ, 3, 2 * RI, HQ), BF16), V((3, 128, HQ), BF16),
            V((NZ, NX, 2 * RI, HQ), BF16), V((NX, 128, HQ), BF16),
            V((SEQ, HQ), F32), V((NX, SEQ, HQ), F32), V((NX, SEQ, HQ), BF16),
            V((NZ, 64, CH), BF16), V((NZ, 16, CH), F32), V((NZ, 64, CH), BF16), V((NZ, 64, CH), BF16),
            V((TXT, CH), F32), V((CH, SEQ), BF16), V((CH, SEQ), BF16),
            V((NZ, NX, RC, HQ), BF16), V((3, NZ, RC, HQ), BF16), V((NJ, NX, SEQ, HJ), BF16),
            V((2, NX, CH, HQ), BF16), V((2, 2, CH, HQ), BF16), V((2, 3, ROWS, HQ), BF16),
            V((4, 4, TXT, HQ), BF16), V((4, 2, 4, TXT, HQ), BF16), V((4, ROWS, HQ), F32),
            dma(4), dma(4), dma(7), dma(7), dma(7), dma(NZ, 2), dma(NZ, 2), dma(2, 2), dma(NZ, 2), dma(2, 2),
            pltpu.SemaphoreType.DMA, dma(NZ, 2), dma(NZ, 2), dma(4), pltpu.SemaphoreType.DMA, dma(NJ, 2), dma(NJ, 2), dma(2, NJ), dma(2, NJ, 2), dma(4), dma(4), dma(15),
        ],
        compiler_params=pltpu.CompilerParams(
            collective_id=0, has_side_effects=True, vmem_limit_bytes=60 * 1024 * 1024
        ),
    )(
        latent_image, latent_text, noise_image, noise_text, up_image, up_text, down_image, down_text,
        modulation, timesteps, skips, text_lengths,
    )
    return pl.pallas_call(
        hand_on, out_shape=(out, out, out, out), in_specs=[any_] * 4, out_specs=(any_,) * 4,
        scratch_shapes=[V((4, ROWS, HQ), F32), dma(4), dma(4)],
    )(*grads)


def solution(mesh):
    placed = (
        P("dp", "col", None),
        P("dp", "col", None),
        P("dp", "col", None),
        P("dp", "col", None),
        P("row", "col"),
        P("row", "col"),
        P("row", "col"),
        P("row", "col"),
        P(),
        P("dp"),
        P("dp"),
        P("dp"),
    )
    grads = P("row", ("col", "dp"))
    return jax.shard_map(
        body, mesh=mesh, in_specs=placed, out_specs=(grads, grads, grads, grads), check_vma=False
    )
```

time: 149 us -> 139 us (0.933)
  Pallas kernels: 145 us -> 138 us
  other arithmetic: 1.68 us -> 0 us
    pallas_call x1, Pallas kernels: 142 us -> 136 us  [body(): pl.pallas_call(kernel, out_shape=(out, out, out, out), in_specs=[any_] *...]
where the time goes in v4:
time: 139 us
  Pallas kernels  138 us (99%)
    pallas_call x1, Pallas kernels, body(): pl.pallas_call(kernel, out_shape=(out, out, out, out), in_specs=[any_] *...  136 us

profile of v4, /device:TPU:1, one launch (start us, length us, event | category | flops | bytes accessed | tf_op | source)
XLA Modules:
  0.0 139.2 jit_solution(17473892305219324512)
XLA Ops:
  0.6 135.9 %shard_map.147 = (f32[384,384]{1,0:T(8,128)}, f32[384,384]{1,0:T(8,128)}, f32[384,384]{1,0:T(8,128)}, f32[384,384]{1,0:T(8,128)}) custom-call(bf16[2,56,3072]{2,1,0:T(8,128)(2,1)} %lat_i.1, bf16[2,8,3072]{2,1,0:T(8,128)(2,1)} %lat_t.1, bf16[2,56,3072]{2,1,0:T(8,128)(2,1)} %noi_i.1, bf16[2,8,3072]{2,1,0:T(8,128)(2,1)} %noi_t.1, bf16[384,1536]{1,0:T(8,128)(2,1)} %up_i.1, ...), custom_call_target="tpu_custom_call" | custom-call | tf_op jit(solution)/shard_map/pallas_call | solution.py:808
  136.6 2.5 %shard_map.148 = (f32[384,384]{1,0:T(8,128)}, f32[384,384]{1,0:T(8,128)}, f32[384,384]{1,0:T(8,128)}, f32[384,384]{1,0:T(8,128)}) custom-call(f32[384,384]{1,0:T(8,128)} %get-tuple-element.8.a, f32[384,384]{1,0:T(8,128)} %get-tuple-element.9.b, f32[384,384]{1,0:T(8,128)} %get-tuple-element.10.c, f32[384,384]{1,0:T(8,128)} %get-tuple-element.11.d), custom_call_target="tpu_custom_call" | custom-call | tf_op jit(solution)/shard_map/pallas_call | solution.py:836

commit v5 on v4

--- a/solution.py
+++ b/solution.py
@@ -753,11 +753,19 @@
             TS[3, q, :, lanes] = text.reshape(TXT, HJ).astype(BF16)
         return lanes
 
-    for j in range(NJ):
+    def up_grad(j):
         lanes = pg_in(j)
         grad(1, j, uT[...], jnp.concatenate([pg[j, q] for q in range(NX)], axis=1))
+        return lanes
+
+    parts = [up_grad(j) for j in range(NJ - 1)]
+    after_core(1, 0)
+    send_text(3, lanes=parts[0])
+    parts.append(up_grad(NJ - 1))
+    for j in range(1, NJ):
         after_core(1, j)
-        send_text(3, lanes=lanes)
+    for j in range(1, NJ):
+        send_text(3, lanes=parts[j])
 
     join_y(1, 0)
     for j in range(NJ):

time: 139 us -> 140 us (level)
  no operation moved by 1% of the time
where the time goes in v5:
time: 140 us
  Pallas kernels  139 us (99%)
    pallas_call x1, Pallas kernels, body(): pl.pallas_call(kernel, out_shape=(out, out, out, out), in_specs=[any_] *...  137 us

profile of v5, /device:TPU:1, one launch (start us, length us, event | category | flops | bytes accessed | tf_op | source)
XLA Modules:
  0.0 140.0 jit_solution(14091738447809957662)
XLA Ops:
  0.6 136.6 %shard_map.147 = (f32[384,384]{1,0:T(8,128)}, f32[384,384]{1,0:T(8,128)}, f32[384,384]{1,0:T(8,128)}, f32[384,384]{1,0:T(8,128)}) custom-call(bf16[2,56,3072]{2,1,0:T(8,128)(2,1)} %lat_i.1, bf16[2,8,3072]{2,1,0:T(8,128)(2,1)} %lat_t.1, bf16[2,56,3072]{2,1,0:T(8,128)(2,1)} %noi_i.1, bf16[2,8,3072]{2,1,0:T(8,128)(2,1)} %noi_t.1, bf16[384,1536]{1,0:T(8,128)(2,1)} %up_i.1, ...), custom_call_target="tpu_custom_call" | custom-call | tf_op jit(solution)/shard_map/pallas_call | solution.py:816
  137.3 2.5 %shard_map.148 = (f32[384,384]{1,0:T(8,128)}, f32[384,384]{1,0:T(8,128)}, f32[384,384]{1,0:T(8,128)}, f32[384,384]{1,0:T(8,128)}) custom-call(f32[384,384]{1,0:T(8,128)} %get-tuple-element.8.a, f32[384,384]{1,0:T(8,128)} %get-tuple-element.9.b, f32[384,384]{1,0:T(8,128)} %get-tuple-element.10.c, f32[384,384]{1,0:T(8,128)} %get-tuple-element.11.d), custom_call_target="tpu_custom_call" | custom-call | tf_op jit(solution)/shard_map/pallas_call | solution.py:844

commit v6 on v4

--- a/solution.py
+++ b/solution.py
@@ -738,26 +738,37 @@
         rs_hg(i).wait()
     for j in range(NJ):
         pre_late(j)
+    def pg_text(part):
+        rows = slice(part * 32, part * 32 + 32)
+        tokens = slice(part * (SEQ // 2), (part + 1) * (SEQ // 2))
+        for q in range(NX):
+            for j in range(NJ):
+                text = pg[j, q, tokens, :].astype(F32).reshape(NZ // 2, RC, HJ)[:, RI:RC]
+                TS[3, q, rows, j * HJ : (j + 1) * HJ] = text.reshape(32, HJ).astype(BF16)
+        send_text(3, rows)
+
+    pass_late(0)
+    join_y(0, 0)
     early = pg.at[:, 0:2, 0 : SEQ // 2]
     remote(early, early, s_sent.at[12], s_pgeg, core).wait_recv()
-    for j in range(NJ):
-        pass_late(j)
-        join_y(0, j)
-
-    def pg_in(j):
+    pass_late(1)
+    pg_text(0)
+    join_y(0, 1)
+    pass_late(2)
+    join_y(0, 2)
+
+    def up_grad(j):
         for h in range(2):
             ag_late(j, h).wait()
-        lanes = slice(j * HJ, (j + 1) * HJ)
-        for q in range(NX):
-            text = pg[j, q].astype(F32).reshape(NZ, RC, HJ)[:, RI:RC]
-            TS[3, q, :, lanes] = text.reshape(TXT, HJ).astype(BF16)
-        return lanes
-
-    for j in range(NJ):
-        lanes = pg_in(j)
         grad(1, j, uT[...], jnp.concatenate([pg[j, q] for q in range(NX)], axis=1))
+
+    for j in range(NJ - 1):
+        up_grad(j)
+    after_core(1, 0)
+    up_grad(NJ - 1)
+    for j in range(1, NJ):
         after_core(1, j)
-        send_text(3, lanes=lanes)
+    pg_text(1)
 
     join_y(1, 0)
     for j in range(NJ):

time: 139 us -> 138 us (level)
    pallas_call x1, Pallas kernels: 136 us -> 135 us  [body(): pl.pallas_call(kernel, out_shape=(out, out, out, out), in_specs=[any_] *...]
where the time goes in v6:
time: 138 us
  Pallas kernels  137 us (99%)
    pallas_call x1, Pallas kernels, body(): pl.pallas_call(kernel, out_shape=(out, out, out, out), in_specs=[any_] *...  135 us

profile of v6, /device:TPU:1, one launch (start us, length us, event | category | flops | bytes accessed | tf_op | source)
XLA Modules:
  0.0 137.8 jit_solution(15462922699667774458)
XLA Ops:
  0.6 134.5 %shard_map.147 = (f32[384,384]{1,0:T(8,128)}, f32[384,384]{1,0:T(8,128)}, f32[384,384]{1,0:T(8,128)}, f32[384,384]{1,0:T(8,128)}) custom-call(bf16[2,56,3072]{2,1,0:T(8,128)(2,1)} %lat_i.1, bf16[2,8,3072]{2,1,0:T(8,128)(2,1)} %lat_t.1, bf16[2,56,3072]{2,1,0:T(8,128)(2,1)} %noi_i.1, bf16[2,8,3072]{2,1,0:T(8,128)(2,1)} %noi_t.1, bf16[384,1536]{1,0:T(8,128)(2,1)} %up_i.1, ...), custom_call_target="tpu_custom_call" | custom-call | tf_op jit(solution)/shard_map/pallas_call | solution.py:819
  135.2 2.5 %shard_map.148 = (f32[384,384]{1,0:T(8,128)}, f32[384,384]{1,0:T(8,128)}, f32[384,384]{1,0:T(8,128)}, f32[384,384]{1,0:T(8,128)}) custom-call(f32[384,384]{1,0:T(8,128)} %get-tuple-element.8.a, f32[384,384]{1,0:T(8,128)} %get-tuple-element.9.b, f32[384,384]{1,0:T(8,128)} %get-tuple-element.10.c, f32[384,384]{1,0:T(8,128)} %get-tuple-element.11.d), custom_call_target="tpu_custom_call" | custom-call | tf_op jit(solution)/shard_map/pallas_call | solution.py:847

commit v7 on v6

--- a/solution.py
+++ b/solution.py
@@ -648,7 +648,7 @@
 
         at(k, 2, pre_early, 0)
         at(k, 3, pre_early, 1)
-        at(k, 3, pre_early, 2)
+        at(k, 4, pre_early, 2)
         at(k, 4, pre_early, 3)
 
         @pl.when(k >= 3)

time: 138 us -> 138 us (level)
  no operation moved by 1% of the time
where the time goes in v7:
time: 138 us
  Pallas kernels  137 us (99%)
    pallas_call x1, Pallas kernels, body(): pl.pallas_call(kernel, out_shape=(out, out, out, out), in_specs=[any_] *...  135 us

profile of v7, /device:TPU:1, one launch (start us, length us, event | category | flops | bytes accessed | tf_op | source)
XLA Modules:
  0.0 137.8 jit_solution(18239573527886798363)
XLA Ops:
  0.6 134.5 %shard_map.147 = (f32[384,384]{1,0:T(8,128)}, f32[384,384]{1,0:T(8,128)}, f32[384,384]{1,0:T(8,128)}, f32[384,384]{1,0:T(8,128)}) custom-call(bf16[2,56,3072]{2,1,0:T(8,128)(2,1)} %lat_i.1, bf16[2,8,3072]{2,1,0:T(8,128)(2,1)} %lat_t.1, bf16[2,56,3072]{2,1,0:T(8,128)(2,1)} %noi_i.1, bf16[2,8,3072]{2,1,0:T(8,128)(2,1)} %noi_t.1, bf16[384,1536]{1,0:T(8,128)(2,1)} %up_i.1, ...), custom_call_target="tpu_custom_call" | custom-call | tf_op jit(solution)/shard_map/pallas_call | solution.py:819
  135.1 2.5 %shard_map.148 = (f32[384,384]{1,0:T(8,128)}, f32[384,384]{1,0:T(8,128)}, f32[384,384]{1,0:T(8,128)}, f32[384,384]{1,0:T(8,128)}) custom-call(f32[384,384]{1,0:T(8,128)} %get-tuple-element.8.a, f32[384,384]{1,0:T(8,128)} %get-tuple-element.9.b, f32[384,384]{1,0:T(8,128)} %get-tuple-element.10.c, f32[384,384]{1,0:T(8,128)} %get-tuple-element.11.d), custom_call_target="tpu_custom_call" | custom-call | tf_op jit(solution)/shard_map/pallas_call | solution.py:847
